TPU v7x, 32 devices: a whole 2x2x4 slice. The times are simulated.
32 devices in a mesh: row: 4 (over z), col: 8 (over y, x, core).
Axes of the slice: x: 2, y: 2, z: 4, core: 2. Of those that a mesh axis runs over, the one named last changes fastest.
Arguments:
- s_slab: bfloat16 [128, 262144], P(None, ('row', 'col')), may hold values from -4 to 4
- p_blocks: bfloat16 [4, 8, 64, 128, 128], P('row', 'col'), may hold values from -0.5 to 0.5
- p_index: int32 [4, 8, 2, 64], P('row', 'col'), may hold values from -1 to 2047, as said below
Outputs:
- purified: bfloat16 [128, 262144], P(None, ('row', 'col'))
Inputs may be any that keep to these rules, and one draw needn't show every extreme that they name: `p_index`: the slot on device (r, c) holds blocks whose block column lies in r * 512 to (r + 1) * 512 - 1 and whose block row k has (k // 64) % 8 == c; no block appears twice; live slots come first in each device's list and both entries of a slot are -1 or both are live; some device has all 64 slots live in every draw.
All inputs are finite; a program needn't handle non-finite values.
Results may differ from a plain program's by a relative error of at most 0.0034.
Values may be sent and summed in bfloat16 or wider, within the bound.
No kernel may reach another device: no remote copies, remote signals or barrier semaphores. Data moves between devices by JAX's collectives and lax.ppermute only.
A program may use at most 192 MiB of HBM per device.

v0:
```python
import jax
import jax.numpy as jnp
from jax import lax
from jax.sharding import PartitionSpec as P


def body(s_slab, p_blocks, p_index):
    blk = s_slab.shape[0]
    per_piece = s_slab.shape[1] // blk
    n_row = lax.axis_size("row")
    n_col = lax.axis_size("col")
    span = n_col * per_piece
    slots = p_blocks.shape[2]
    group = min(64, slots)
    gathered = lax.all_gather(s_slab, "row", axis=1, tiled=True)
    panels = gathered.reshape(blk, n_row * per_piece, blk)
    stored = p_blocks[0, 0]
    block_rows = p_index[0, 0, 0]
    block_cols = p_index[0, 0, 1]
    local_rows = jnp.clip(
        block_rows // per_piece // n_col * per_piece + block_rows % per_piece,
        0,
        n_row * per_piece - 1,
    )
    row_here = lax.axis_index("row")
    local_cols = jnp.where(block_cols >= 0, block_cols - row_here * span, span)

    def add_group(number, total):
        taken = jnp.take(panels, local_rows, axis=1)
        product = jnp.einsum("agk,gkb->gab", taken, stored, preferred_element_type=jnp.float32)
        inside = (local_cols >= 0) & (local_cols < 0 + span)
        target = jnp.where(inside, local_cols - 0, span)
        return total + jax.ops.segment_sum(product, target, num_segments=span)

    start = jnp.zeros((span, blk, blk), jnp.float32)
    cube = lax.psum_scatter(
        lax.fori_loop(0, slots // group, add_group, start).astype(jnp.bfloat16),
        "col",
        scatter_dimension=0,
        tiled=True,
    ).astype(jnp.float32)
    cube = cube.transpose(1, 0, 2).reshape(blk, per_piece * blk)
    return (3.0 * s_slab.astype(jnp.float32) - 2.0 * cube).astype(jnp.bfloat16)


def solution(mesh):
    placed = (
        P(None, ("row", "col")),
        P("row", "col", None, None, None),
        P("row", "col", None, None),
    )
    return jax.shard_map(
        body, mesh=mesh, in_specs=placed, out_specs=P(None, ("row", "col")), check_vma=False
    )
```

profile of v0, /device:TPU:0, one launch (start us, length us, event | category | flops | bytes accessed | tf_op | source)
XLA Modules:
  0.0 367.5 jit_solution(8390687752779509310)
XLA Ops:
  6.5 0.0 copy-start
  6.5 0.0 copy-start.2
  6.5 0.0 all-gather.2.cloned.1.call-start
  6.5 4.2 %copy.4 = bf16[128,8192]{0,1:T(8,128)(2,1)} copy(bf16[128,8192]{1,0:T(8,128)(2,1)} %param.3) | data formatting | bytes 4194304 | tf_op args[0]
  10.8 0.0 all-gather.2.cloned.1.call-update
  10.8 0.0 reduce-scatter.2.cloned.1.call-start
  10.8 0.0 copy-done.2
  10.9 152.4 %all-gather.2.cloned.1.call-done = bf16[128,32768]{0,1:T(8,128)(2,1)} async-done(((bf16[128,8192]{0,1:T(8,128)(2,1)}), bf16[128,32768]{0,1:T(8,128)(2,1)}) %all-gather.2.cloned.1.call-update) | async-done | bytes 8388624 | tf_op jit(solution)/shard_map/all_gather | solution.py:15
  163.3 12.0 %copy.6 = bf16[128,256,128]{2,0,1:T(8,128)(2,1)} copy(bf16[128,256,128]{0,2,1:T(8,128)(2,1)} %bitcast.53) | data formatting | bytes 16777216 | tf_op jit(solution)/shard_map/reshape | solution.py:16
  175.2 5.5 %gather_fusion = bf16[64,128,128]{2,1,0:T(8,128)(2,1)} fusion(bf16[128,256,128]{2,0,1:T(8,128)(2,1)} %copy.6, s32[1024]{0:T(1024)S(1)} %pad_clamp_fusion), kind=kCustom, calls=%fused_computation | custom fusion | bytes 4194560 | tf_op jit(solution)/shard_map/while/body/eval_jaxpr/jit(_take)/gather | solution.py:29
  180.8 0.0 copy-done
  180.8 4.4 %fusion.1 = f32[64,128,128]{2,1,0:T(8,128)} fusion(bf16[1,1,64,128,128]{4,3,2,1,0:T(8,128)(2,1)S(1)} %copy-done, bf16[64,128,128]{2,1,0:T(8,128)(2,1)} %gather_fusion, pred[64]{0:T(512)(128)(4,1)S(1)} %compare_and_fusion), kind=kOutput, calls=%fused_computation.5 | convolution fusion | flops 269484032 | bytes 8388672 | tf_op jit(solution)/shard_map/while/body/eval_jaxpr/agk,gkb->gab/dot_general | solution.py:30
  185.2 11.2 %broadcast.273 = f32[512,128,128]{2,1,0:T(8,128)} broadcast(f32[]{:T(128)} %constant.72.clone.1), dimensions={} | broadcast | bytes 33554436 | tf_op jit(solution)/shard_map/broadcast.10
  196.4 13.1 %scatter_fusion = f32[512,128,128]{2,1,0:T(8,128)} fusion(f32[512,128,128]{2,1,0:T(8,128)} %broadcast.273, s32[64]{0:T(128)S(1)} %get-tuple-element.16, f32[64,128,128]{2,1,0:T(8,128)} %fusion.1), kind=kCustom, calls=%fused_computation.1 | custom fusion | flops 1048576 | bytes 12583168 | tf_op jit(solution)/shard_map/while/body/eval_jaxpr/scatter-add | solution.py:33
  209.6 17.7 %convert_element_type.13 = bf16[512,128,128]{2,1,0:T(8,128)(2,1)} convert(f32[512,128,128]{2,1,0:T(8,128)} %scatter_fusion) | non-fusion elementwise | flops 8388608 | bytes 50331648 | tf_op jit(solution)/shard_map/convert_element_type | solution.py:37
  227.3 0.0 reduce-scatter.2.cloned.1.call-update
  227.3 114.7 %reduce-scatter.2.cloned.1.call-done = bf16[64,128,128]{2,1,0:T(8,128)(2,1)} async-done(((bf16[512,128,128]{2,1,0:T(8,128)(2,1)}), bf16[64,128,128]{2,1,0:T(8,128)(2,1)}) %reduce-scatter.2.cloned.1.call-update) | async-done | bytes 2097168 | tf_op jit(solution)/shard_map/reduce_scatter | solution.py:36
  342.0 4.1 %multiply_bitcast_fusion = f32[128,64,128]{2,0,1:T(8,128)} fusion(bf16[64,128,128]{2,1,0:T(8,128)(2,1)} %reduce-scatter.2.cloned.1.call-done), kind=kLoop, calls=%fused_computation.4 | loop fusion | flops 2097152 | bytes 6291456 | tf_op jit(solution)/shard_map/mul | solution.py:43
  346.1 5.6 %copy.7 = f32[128,64,128]{0,2,1:T(8,128)} copy(f32[128,64,128]{2,0,1:T(8,128)} %multiply_bitcast_fusion) | data formatting | bytes 8388608 | tf_op jit(solution)/shard_map/mul | solution.py:43
  351.7 0.0 copy-start.1
  351.7 4.9 %fusion = bf16[128,8192]{0,1:T(8,128)(2,1)} fusion(f32[128,64,128]{0,2,1:T(8,128)} %copy.7, bf16[128,8192]{0,1:T(8,128)(2,1)} %copy.4), kind=kLoop, calls=%fused_computation.3 | loop fusion | flops 4194304 | bytes 8388608 | tf_op jit(solution)/shard_map/convert_element_type | solution.py:43
  356.6 4.1 %copy.8 = bf16[128,8192]{1,0:T(8,128)(2,1)} copy(bf16[128,8192]{0,1:T(8,128)(2,1)} %fusion) | data formatting | bytes 4194304 | tf_op jit(solution)/shard_map/convert_element_type | solution.py:43
  360.6 0.0 copy-done.1
  (3 shorter events, 0.1 us)
Async XLA Ops:
  6.5 174.2 %copy-start = (bf16[1,1,64,128,128]{4,3,2,1,0:T(8,128)(2,1)S(1)}, bf16[1,1,64,128,128]{4,3,2,1,0:T(8,128)(2,1)}, u32[]{:S(2)}) copy-start(bf16[1,1,64,128,128]{4,3,2,1,0:T(8,128)(2,1)} %param.4) | copy-start | bytes 6291460
  6.5 4.3 %copy-start.2 = (s32[1,1,2,64]{3,2,1,0:T(2,128)S(1)}, s32[1,1,2,64]{3,2,1,0:T(2,128)}, u32[]{:S(2)}) copy-start(s32[1,1,2,64]{3,2,1,0:T(2,128)} %param.5) | copy-start | bytes 1540
  6.5 156.7 %all-gather.2.cloned.1.call-start = ((), (), s32[]{:S(2)}) async-start(), calls=%async_computation.1 | async-start | bytes 10485760 | tf_op jit(solution)/shard_map/all_gather | solution.py:15
  10.8 331.2 %reduce-scatter.2.cloned.1.call-start = ((), (), s32[]{:S(2)}) async-start(), calls=%async_computation.2 | async-start | bytes 18874368 | tf_op jit(solution)/shard_map/reduce_scatter | solution.py:36
  351.7 8.9 %copy-start.1 = (bf16[1,1,64,128,128]{4,3,2,1,0:T(8,128)(2,1)S(1)}, bf16[1,1,64,128,128]{4,3,2,1,0:T(8,128)(2,1)}, u32[]{:S(2)}) copy-start(bf16[1,1,64,128,128]{4,3,2,1,0:T(8,128)(2,1)} %param.4) | copy-start | bytes 6291460
Sparse Core Ops, SparseCore 0:
  10.9 152.3 all-gather.1
  227.4 114.5 reduce-scatter.1
where the time goes:
time: 368 us; the launch traced here: 367 us
  waiting for transfers between devices  267 us (73%)
  local copies, waits for them, and re-layouts  42.6 us (12%)
  other arithmetic  39.9 us (11%)
  between operations  13.4 us (4%)
  matrix products  4.41 us (1%)
    all_gather x1, waiting for transfers between devices, body(): gathered = lax.all_gather(s_slab, 'row', axis=1, tiled=True)  152 us
    reduce_scatter x1, waiting for transfers between devices, body(): lax.psum_scatter(lax.fori_loop(0, slots // group, add_group, start).astyp...  115 us
    convert_element_type x1, other arithmetic, body(): lax.fori_loop(0, slots // group, add_group, start).astype(jnp.bfloat16)  17.7 us
    scatter-add x1, other arithmetic, add_group(): return total + jax.ops.segment_sum(product, target, num_segments=span)  13.1 us
    reshape x1, local copies, waits for them, and re-layouts, body(): panels = gathered.reshape(blk, n_row * per_piece, blk)  12 us
    another operation x1, local copies, waits for them, and re-layouts  11.2 us
  transfers between devices with their start and end apart: 2, of which 2 were waited for; matrix products, arithmetic and copies ran while one was open for 0% of the time, Pallas kernels for 0%

commit v1 on v0

v1 whole, which is shorter than its diff:
```python
import jax
import jax.numpy as jnp
from jax import lax
from jax.experimental import pallas as pl
from jax.experimental.pallas import tpu as pltpu
from jax.sharding import PartitionSpec as P

CAP_ROW = 24
CAP_COL = 16
PARTS = 2
VMEM_LIMIT = 60 * 1024 * 1024


def smem():
    return pl.BlockSpec(memory_space=pltpu.SMEM)


def anywhere():
    return pl.BlockSpec(memory_space=pl.ANY)


def pairs(n, t):
    return [(i, i ^ t) for i in range(n)]


def ask_kernel(n_row, n_col, per_piece, cap, base, index, *refs):
    asks, place, most = refs[:n_row], refs[n_row], refs[n_row + 1]
    mark, table, count, start = refs[n_row + 2 :]
    slots = index.shape[1]
    row = lax.axis_index("row")
    for t in range(n_row):
        count[t] = 0
        start[t] = base[t]

    def where(s):
        k = jnp.maximum(index[0, s], 0)
        return lax.div(k, per_piece * n_col), lax.rem(k, per_piece)

    def clear(s, carry):
        owner, panel = where(s)
        mark[owner * per_piece + panel] = -1
        return carry

    lax.fori_loop(0, slots, clear, 0, unroll=8)

    def step(s, carry):
        owner, panel = where(s)
        spot = owner * per_piece + panel
        t = owner ^ row
        seen = mark[spot]
        fresh = (index[0, s] >= 0) & (seen < 0)
        held = count[t]
        at = jnp.where(seen < 0, held, seen)

        @pl.when(fresh)
        def _():
            mark[spot] = held
            table[t, held] = panel
            count[t] = held + 1

        limit = jnp.where(t == 0, table.shape[1], cap)
        place[0, s] = start[t] + jnp.minimum(at, limit - 1)
        return carry + jnp.where(index[0, s] >= 0, 1, 0)

    live = lax.fori_loop(0, slots, step, 0)
    largest = 0
    for t in range(n_row):
        asks[t][0, 0] = count[t]
        if t > 0:
            largest = jnp.maximum(largest, count[t])

        def copy(i, carry):
            asks[t][0, 1 + i] = table[t, i]
            return carry

        lax.fori_loop(0, count[t], copy, 0)
    most[0, 0] = largest
    most[0, 1] = live


def plan_kernel(n_col, per_piece, cap, base, trash, index, lists, place, most, mark, count, start):
    slots = index.shape[1]
    col = lax.axis_index("col")
    for t in range(n_col):
        count[t] = 0
        start[t] = base[t]

    def where(s):
        j = jnp.maximum(index[1, s], 0)
        piece = lax.div(j, per_piece)
        return lax.rem(piece, n_col), j - piece * per_piece

    def clear(s, carry):
        owner, panel = where(s)
        mark[owner * per_piece + panel] = -1
        return carry

    lax.fori_loop(0, slots, clear, 0, unroll=8)

    def step(s, carry):
        owner, panel = where(s)
        spot = owner * per_piece + panel
        t = owner ^ col
        seen = mark[spot]
        alive = index[1, s] >= 0
        fresh = alive & (seen < 0)
        held = count[t]
        at = jnp.where(seen < 0, held, seen)

        @pl.when(fresh)
        def _():
            mark[spot] = held
            lists[owner, 1 + held] = panel
            count[t] = held + 1

        limit = jnp.where(t == 0, min(per_piece, slots), cap)
        spot_out = start[t] + jnp.minimum(at, limit - 1)
        place[0, s] = jnp.where(alive, spot_out, trash)
        place[1, s] = jnp.where(fresh, 1, 0)
        return carry

    lax.fori_loop(0, slots, step, 0)
    largest = 0
    for t in range(n_col):
        lists[col ^ t, 0] = count[t]
        if t > 0:
            largest = jnp.maximum(largest, count[t])
    most[0, 0] = largest


def pack_kernel(blk, *refs):
    n_row = (len(refs) - 1) // 2
    asks, slab, packs = refs[:n_row], refs[n_row], refs[n_row + 1 :]
    for ask, pack in zip(asks, packs):

        def copy(i, carry):
            at = pl.multiple_of(ask[0, 1 + i] * blk, blk)
            pack[i] = slab[:, pl.ds(at, blk)]
            return carry

        lax.fori_loop(0, jnp.minimum(ask[0, 0], pack.shape[0]), copy, 0)


def product_kernel(n_row, n_col, base_in, base_out, group, place_in, place_out, most, lists, stored, *refs):
    panels, sums = refs[:n_row], refs[n_row : n_row + n_col]
    held, total, sems = refs[n_row + n_col :]
    copies = [
        pltpu.make_async_copy(panel, held.at[pl.ds(base_in[t], panel.shape[0])], sems.at[t])
        for t, panel in enumerate(panels)
    ]
    for copy in copies:
        copy.start()
    for copy in copies:
        copy.wait()
    live = most[0, 1]

    def step(g, carry):
        products = []
        for u in range(group):
            s = g * group + u
            products.append(
                jnp.dot(held[place_in[0, s]], stored[s], preferred_element_type=jnp.float32)
            )
        for u in range(group):
            s = g * group + u
            o = place_out[0, s]
            before = jnp.where(place_out[1, s] == 1, 0.0, total[o])
            total[o] = before + products[u]
        return carry

    lax.fori_loop(0, lax.div(live + group - 1, group), step, 0)
    col = lax.axis_index("col")
    for t in range(n_col):

        def store(i, carry):
            sums[t][i] = total[base_out[t] + i].astype(jnp.bfloat16)
            return carry

        lax.fori_loop(0, jnp.minimum(lists[col ^ t, 0], sums[t].shape[0]), store, 0)


def combine_kernel(n_col, blk, lists, slab, *refs):
    sums, out, total = refs[:n_col], refs[-2], refs[-1]
    col = lax.axis_index("col")
    pieces = out.shape[1] // blk
    total[...] = jnp.zeros_like(total)
    for t in range(n_col):
        source = col ^ t

        def add(i, carry):
            at = lists[source, 1 + i]
            total[at] += sums[t][i].astype(jnp.float32)
            return carry

        lax.fori_loop(0, jnp.minimum(lists[source, 0], sums[t].shape[0]), add, 0)
    for i in range(pieces):
        here = pl.ds(i * blk, blk)
        out[:, here] = (3.0 * slab[:, here].astype(jnp.float32) - 2.0 * total[i]).astype(out.dtype)


def dense(s_slab, p_blocks, p_index):
    blk = s_slab.shape[0]
    per_piece = s_slab.shape[1] // blk
    n_row = lax.axis_size("row")
    n_col = lax.axis_size("col")
    span = n_col * per_piece
    gathered = lax.all_gather(s_slab, "row", axis=1, tiled=True)
    panels = gathered.reshape(blk, n_row * per_piece, blk)
    block_rows = p_index[0, 0, 0]
    block_cols = p_index[0, 0, 1]
    local_rows = jnp.clip(
        block_rows // per_piece // n_col * per_piece + block_rows % per_piece,
        0,
        n_row * per_piece - 1,
    )
    local_cols = jnp.where(block_cols >= 0, block_cols - lax.axis_index("row") * span, span)
    taken = jnp.take(panels, local_rows, axis=1)
    product = jnp.einsum("agk,gkb->gab", taken, p_blocks[0, 0], preferred_element_type=jnp.float32)
    term = jax.ops.segment_sum(product, local_cols, num_segments=span)
    cube = lax.psum_scatter(term.astype(jnp.bfloat16), "col", scatter_dimension=0, tiled=True)
    cube = cube.astype(jnp.float32).transpose(1, 0, 2).reshape(blk, per_piece * blk)
    return (3.0 * s_slab.astype(jnp.float32) - 2.0 * cube).astype(jnp.bfloat16)


def body(s_slab, p_blocks, p_index):
    blk = s_slab.shape[0]
    per_piece = s_slab.shape[1] // blk
    n_row = lax.axis_size("row")
    n_col = lax.axis_size("col")
    slots = p_blocks.shape[2]
    stored = p_blocks[0, 0]
    index = p_index[0, 0]
    full = min(per_piece, slots)
    cap_row = min(CAP_ROW, full)
    cap_col = min(CAP_COL, full)
    wide = -(-(1 + full) // 128) * 128
    caps_in = [full] + [cap_row] * (n_row - 1)
    caps_out = [full] + [cap_col] * (n_col - 1)
    base_in = [sum(caps_in[:t]) for t in range(n_row)]
    base_out = [sum(caps_out[:t]) for t in range(n_col)]
    trash = sum(caps_out)
    parts = PARTS if blk % (16 * PARTS) == 0 else 1
    rows = blk // parts
    group = 4 if slots % 4 == 0 else 1
    params = pltpu.CompilerParams(vmem_limit_bytes=VMEM_LIMIT)
    table = jax.ShapeDtypeStruct((1, wide), jnp.int32)

    asked = pl.pallas_call(
        lambda *refs: ask_kernel(n_row, n_col, per_piece, cap_row, base_in, *refs),
        out_shape=[table] * n_row + [jax.ShapeDtypeStruct((1, slots), jnp.int32), table],
        in_specs=[smem()],
        out_specs=[smem()] * (n_row + 2),
        scratch_shapes=[
            pltpu.SMEM((n_row * per_piece,), jnp.int32),
            pltpu.SMEM((n_row, full), jnp.int32),
            pltpu.SMEM((n_row,), jnp.int32),
            pltpu.SMEM((n_row,), jnp.int32),
        ],
        name="ask",
    )(index)
    asks, place_in, most_in = asked[:n_row], asked[n_row], asked[n_row + 1]
    asks = [asks[0]] + [lax.ppermute(asks[t], "row", pairs(n_row, t)) for t in range(1, n_row)]

    lists, place_out, most_out = pl.pallas_call(
        lambda *refs: plan_kernel(n_col, per_piece, cap_col, base_out, trash, *refs),
        out_shape=[
            jax.ShapeDtypeStruct((n_col, wide), jnp.int32),
            jax.ShapeDtypeStruct((2, slots), jnp.int32),
            table,
        ],
        in_specs=[smem()],
        out_specs=[smem()] * 3,
        scratch_shapes=[
            pltpu.SMEM((n_col * per_piece,), jnp.int32),
            pltpu.SMEM((n_col,), jnp.int32),
            pltpu.SMEM((n_col,), jnp.int32),
        ],
        name="plan",
    )(index)
    arriving = lax.all_to_all(lists, "col", 0, 0, tiled=True)

    packed = []
    for part in range(parts):
        packed.append(
            pl.pallas_call(
                lambda *refs: pack_kernel(blk, *refs),
                grid=(1,),
                out_shape=[jax.ShapeDtypeStruct((cap, rows, blk), jnp.bfloat16) for cap in caps_in],
                in_specs=[smem()] * n_row
                + [pl.BlockSpec((rows, s_slab.shape[1]), lambda i, part=part: (part, 0))],
                out_specs=[pl.BlockSpec((cap, rows, blk), lambda i: (0, 0, 0)) for cap in caps_in],
                compiler_params=params,
                cost_estimate=pl.CostEstimate(
                    flops=0, bytes_accessed=2 * s_slab.size * 2 // parts, transcendentals=0
                ),
                name="pack",
            )(*asks, s_slab)
        )
    fetched = [
        [packed[part][0]]
        + [lax.ppermute(packed[part][t], "row", pairs(n_row, t)) for t in range(1, n_row)]
        for part in range(parts)
    ]
    sums = []
    for part in range(parts):
        done = pl.pallas_call(
            lambda *refs: product_kernel(n_row, n_col, base_in, base_out, group, *refs),
            out_shape=[jax.ShapeDtypeStruct((cap, rows, blk), jnp.bfloat16) for cap in caps_out],
            in_specs=[smem()] * 4
            + [pl.BlockSpec(memory_space=pltpu.VMEM)]
            + [anywhere()] * n_row,
            out_specs=[pl.BlockSpec(memory_space=pltpu.VMEM)] * n_col,
            scratch_shapes=[
                pltpu.VMEM((sum(caps_in), rows, blk), jnp.bfloat16),
                pltpu.VMEM((trash + 1, rows, blk), jnp.float32),
                pltpu.SemaphoreType.DMA((n_row,)),
            ],
            compiler_params=params,
            cost_estimate=pl.CostEstimate(
                flops=2 * slots * rows * blk * blk,
                bytes_accessed=2 * blk * blk * slots + 2 * rows * blk * (sum(caps_in) + trash),
                transcendentals=0,
            ),
            name="product",
        )(place_in, place_out, most_in, lists, stored, *fetched[part])
        sums.append(
            [done[0]] + [lax.ppermute(done[t], "col", pairs(n_col, t)) for t in range(1, n_col)]
        )

    def combine(part, before):
        extra = [] if before is None else [before]
        return pl.pallas_call(
            lambda *refs: combine_kernel(n_col, blk, *refs),
            grid=(1,),
            out_shape=jax.ShapeDtypeStruct(s_slab.shape, s_slab.dtype),
            in_specs=[smem()]
            + [pl.BlockSpec((rows, s_slab.shape[1]), lambda i: (part, 0))]
            + [pl.BlockSpec((cap, rows, blk), lambda i: (0, 0, 0)) for cap in caps_out]
            + [anywhere()] * len(extra),
            out_specs=pl.BlockSpec((rows, s_slab.shape[1]), lambda i: (part, 0)),
            scratch_shapes=[pltpu.VMEM((per_piece, rows, blk), jnp.float32)],
            input_output_aliases={2 + n_col: 0} if extra else {},
            compiler_params=params,
            cost_estimate=pl.CostEstimate(
                flops=4 * s_slab.size // parts,
                bytes_accessed=4 * s_slab.size // parts + 2 * rows * blk * trash,
                transcendentals=0,
            ),
            name="combine",
        )(arriving, s_slab, *sums[part], *extra)

    result = None
    for part in range(parts - 1):
        result = combine(part, result)
    if cap_row == full and cap_col == full:
        return combine(parts - 1, result)
    over = jnp.maximum(most_in[0, 0] - cap_row, most_out[0, 0] - cap_col)
    over = lax.pmax(over, ("row", "col"))
    return lax.cond(
        over > 0,
        lambda: dense(s_slab, p_blocks, p_index),
        lambda: combine(parts - 1, result),
    )


def solution(mesh):
    placed = (
        P(None, ("row", "col")),
        P("row", "col", None, None, None),
        P("row", "col", None, None),
    )
    return jax.shard_map(
        body, mesh=mesh, in_specs=placed, out_specs=P(None, ("row", "col")), check_vma=False
    )
```

time: 368 us -> 184 us (0.50)
  waiting for transfers between devices: 267 us -> 56.1 us
  blocking collectives: 0 us -> 47.3 us
  local copies, waits for them, and re-layouts: 42.6 us -> 2.12 us
  other arithmetic: 39.9 us -> 0 us
  starting transfers between devices: 0.04 us -> 34.5 us
  Pallas kernels: 0 us -> 29.6 us
  matrix products: 4.41 us -> 0 us
    all_gather x1 -> x0, waiting for transfers between devices: 152 us -> none  [body(): gathered = lax.all_gather(s_slab, 'row', axis=1, tiled=True)]
    reduce_scatter x1 -> x0, waiting for transfers between devices: 115 us -> none  [body(): lax.psum_scatter(lax.fori_loop(0, slots // group, add_group, start).astyp...]
    ppermute x0 -> x23, waiting for transfers between devices: none -> 56.1 us  [the longest x6 43.7 us: body(): lax.ppermute(packed[part][t], 'row', pairs(n_row, t))]
    pmax x0 -> x1, blocking collectives: none -> 47.3 us  [body(): over = lax.pmax(over, ('row', 'col'))]
    ppermute x0 -> x23, starting transfers between devices: none -> 31.2 us  [the longest x14 19.2 us: body(): lax.ppermute(done[t], 'col', pairs(n_col, t))]
    pallas_call x0 -> x8, Pallas kernels: none -> 29.6 us  [the longest x2 11.5 us: body(): pl.pallas_call(lambda *refs: product_kernel(n_row, n_col, base_in, base_o...]
    convert_element_type x2 -> x0, other arithmetic: 22.6 us -> none  [the longest x1 17.7 us: body(): lax.fori_loop(0, slots // group, add_group, start).astype(jnp.bfloat16)]
    scatter-add x1 -> x0, other arithmetic: 13.1 us -> none  [add_group(): return total + jax.ops.segment_sum(product, target, num_segments=span)]
  transfers between devices with their start and end apart: 2 -> 24, of which waited for: 2 -> 7; matrix products, arithmetic and copies ran while one was open for 0% -> 0% of each run, Pallas kernels for 0% -> 11%
where the time goes in v1:
time: 184 us
  waiting for transfers between devices  56.1 us (30%)
  blocking collectives  47.3 us (26%)
  starting transfers between devices  34.5 us (19%)
  Pallas kernels  29.6 us (16%)
  between operations  14.3 us (8%)
  local copies, waits for them, and re-layouts  2.12 us (1%)
    pmax x1, blocking collectives, body(): over = lax.pmax(over, ('row', 'col'))  47.3 us
    ppermute x6, waiting for transfers between devices, body(): lax.ppermute(packed[part][t], 'row', pairs(n_row, t))  43.7 us
    ppermute x14, starting transfers between devices, body(): lax.ppermute(done[t], 'col', pairs(n_col, t))  19.2 us
    pallas_call x2, Pallas kernels, body(): pl.pallas_call(lambda *refs: product_kernel(n_row, n_col, base_in, base_o...  11.5 us
    ppermute x14, waiting for transfers between devices, body(): lax.ppermute(done[t], 'col', pairs(n_col, t))  6.92 us
    pallas_call x2, Pallas kernels, combine(): pl.pallas_call(lambda *refs: combine_kernel(n_col, blk, *refs), grid=(1,)...  6.68 us
    ppermute x6, starting transfers between devices, body(): lax.ppermute(packed[part][t], 'row', pairs(n_row, t))  6.11 us
    ppermute x3, starting transfers between devices, body(): lax.ppermute(asks[t], 'row', pairs(n_row, t))  5.87 us
  transfers between devices with their start and end apart: 24, of which 7 were waited for; matrix products, arithmetic and copies ran while one was open for 0% of the time, Pallas kernels for 11%

profile of v1, /device:TPU:0, one launch (start us, length us, event | category | flops | bytes accessed | tf_op | source)
XLA Modules:
  0.0 183.9 jit_solution(17760282713649361480)
XLA Ops:
  6.5 3.0 %ask.1 = (s32[1,128]{1,0:T(1,128)}, s32[1,128]{1,0:T(1,128)}, s32[1,128]{1,0:T(1,128)}, s32[1,128]{1,0:T(1,128)}, s32[1,64]{1,0:T(1,128)}, /*index=5*/s32[1,128]{1,0:T(1,128)}) custom-call(s32[2,64]{1,0:T(2,128)} %bitcast.62), custom_call_target="tpu_custom_call" | custom-call | tf_op jit(solution)/shard_map/ask/pallas_call | solution.py:248
  9.6 3.1 %collective-permute-start = (s32[1,128]{1,0:T(1,128)}, s32[1,128]{1,0:T(1,128)S(1)}, u32[]{:S(2)}, u32[]{:S(2)}) collective-permute-start(s32[1,128]{1,0:T(1,128)} %get-tuple-element.89), channel_id=1, source_target_pairs={{0,8},{8,0},{16,24},{24,16},{1,9},{9,1},{17,25},{25,17},{2,10},{10... | collective-permute-start | bytes 1544 | tf_op jit(solution)/shard_map/ppermute | solution.py:262
  12.6 2.8 %collective-permute-start.1 = (s32[1,128]{1,0:T(1,128)}, s32[1,128]{1,0:T(1,128)S(1)}, u32[]{:S(2)}, u32[]{:S(2)}) collective-permute-start(s32[1,128]{1,0:T(1,128)} %get-tuple-element.90), channel_id=1, source_target_pairs={{0,16},{8,24},{16,0},{24,8},{1,17},{9,25},{17,1},{25,9},{2,18},{10... | collective-permute-start | bytes 1544 | tf_op jit(solution)/shard_map/ppermute | solution.py:262
  15.4 1.8 collective-permute-done.1.refs_2_
  17.3 3.7 %collective-permute-done.2.refs_3_ = s32[1,128]{1,0:T(1,128)S(1)} collective-permute-done((s32[1,128]{1,0:T(1,128)}, s32[1,128]{1,0:T(1,128)S(1)}, u32[]{:S(2)}, u32[]{:S(2)}) %collective-permute-start.2) | collective-permute-done | bytes 544 | tf_op jit(solution)/shard_map/ppermute | solution.py:262
  21.6 3.0 %pack.3 = (bf16[64,64,128]{2,1,0:T(8,128)(2,1)}, bf16[24,64,128]{2,1,0:T(8,128)(2,1)}, bf16[24,64,128]{2,1,0:T(8,128)(2,1)}, bf16[24,64,128]{2,1,0:T(8,128)(2,1)}) custom-call(s32[1,128]{1,0:T(1,128)} %get-tuple-element.88.refs_0_, s32[1,128]{1,0:T(1,128)} %copy-done.12, s32[1,128]{1,0:T(1,128)} %copy-done.13, s32[1,128]{1,0:T(1,128)} %copy-done.14, ...), custom_call_target="tpu_custom_call" | custom-call | bytes 2097152 | tf_op jit(solution)/shard_map/pack/pallas_call | solution.py:285
  25.0 4.0 %collective-permute-start.15 = (bf16[24,64,128]{2,1,0:T(8,128)(2,1)}, bf16[24,64,128]{2,1,0:T(8,128)(2,1)}, u32[]{:S(2)}, u32[]{:S(2)}) collective-permute-start(bf16[24,64,128]{2,1,0:T(8,128)(2,1)} %get-tuple-element.107), channel_id=1, source_target_pairs={{0,24},{8,16},{16,8},{24,0},{1,25},{9,17},{17,9},{25,1},{2,26},{10... | collective-permute-start | bytes 1179656 | tf_op jit(solution)/shard_map/ppermute | solution.py:301
  29.0 2.4 %pack.2 = (bf16[64,64,128]{2,1,0:T(8,128)(2,1)}, bf16[24,64,128]{2,1,0:T(8,128)(2,1)}, bf16[24,64,128]{2,1,0:T(8,128)(2,1)}, bf16[24,64,128]{2,1,0:T(8,128)(2,1)}) custom-call(s32[1,128]{1,0:T(1,128)} %get-tuple-element.88.refs_0_, s32[1,128]{1,0:T(1,128)} %copy-done.12, s32[1,128]{1,0:T(1,128)} %copy-done.13, s32[1,128]{1,0:T(1,128)} %copy-done.14, ...), custom_call_target="tpu_custom_call" | custom-call | bytes 2097152 | tf_op jit(solution)/shard_map/pack/pallas_call | solution.py:285
  31.8 11.5 %collective-permute-done.13.refs_6_ = bf16[24,64,128]{2,1,0:T(8,128)(2,1)S(1)} collective-permute-done((bf16[24,64,128]{2,1,0:T(8,128)(2,1)}, bf16[24,64,128]{2,1,0:T(8,128)(2,1)S(1)}, u32[]{:S(2)}, u32[]{:S(2)}) %collective-permute-start.13) | collective-permute-done | bytes 393248 | tf_op jit(solution)/shard_map/ppermute | solution.py:301
  45.3 2.9 %plan.1 = (s32[8,128]{1,0:T(8,128)}, s32[2,64]{1,0:T(2,128)}, s32[1,128]{1,0:T(1,128)}) custom-call(s32[2,64]{1,0:T(2,128)S(1)} %bitcast.63), custom_call_target="tpu_custom_call" | custom-call | tf_op jit(solution)/shard_map/plan/pallas_call | solution.py:264
  48.3 6.5 %collective-permute-done.14.refs_7_ = bf16[24,64,128]{2,1,0:T(8,128)(2,1)} collective-permute-done((bf16[24,64,128]{2,1,0:T(8,128)(2,1)}, bf16[24,64,128]{2,1,0:T(8,128)(2,1)}, u32[]{:S(2)}, u32[]{:S(2)}) %collective-permute-start.14) | collective-permute-done | bytes 393248 | tf_op jit(solution)/shard_map/ppermute | solution.py:301
  54.7 5.9 %product.3 = (bf16[64,64,128]{2,1,0:T(8,128)(2,1)}, bf16[16,64,128]{2,1,0:T(8,128)(2,1)}, bf16[16,64,128]{2,1,0:T(8,128)(2,1)}, bf16[16,64,128]{2,1,0:T(8,128)(2...) custom-call(s32[1,64]{1,0:T(1,128)} %get-tuple-element.86.refs_0_, ...), custom_call_target="tpu_custom_call" | custom-call | flops 134217728 | bytes 7208960 | tf_op jit(solution)/shard_map/product/pallas_call | solution.py:306
  62.6 25.7 %collective-permute-done.4.refs_7_ = bf16[24,64,128]{2,1,0:T(8,128)(2,1)S(1)} collective-permute-done((bf16[24,64,128]{2,1,0:T(8,128)(2,1)}, bf16[24,64,128]{2,1,0:T(8,128)(2,1)S(1)}, u32[]{:S(2)}, u32[]{:S(2)}) %collective-permute-start.4) | collective-permute-done | bytes 393248 | tf_op jit(solution)/shard_map/ppermute | solution.py:301
  90.3 5.6 %product.2 = (bf16[64,64,128]{2,1,0:T(8,128)(2,1)S(1)}, bf16[16,64,128]{2,1,0:T(8,128)(2,1)}, bf16[16,64,128]{2,1,0:T(8,128)(2,1)}, bf16[16,64,128]{2,1,0:T(8,12...) custom-call(s32[1,64]{1,0:T(1,128)} %get-tuple-element.86.refs_0_, ...), custom_call_target="tpu_custom_call" | custom-call | flops 134217728 | bytes 7208960 | tf_op jit(solution)/shard_map/product/pallas_call | solution.py:306
  95.9 1.8 collective-permute-start.21
  101.3 4.9 %collective-permute-done.21.refs_8_ = bf16[16,64,128]{2,1,0:T(8,128)(2,1)S(1)} collective-permute-done((bf16[16,64,128]{2,1,0:T(8,128)(2,1)}, bf16[16,64,128]{2,1,0:T(8,128)(2,1)S(1)}, u32[]{:S(2)}, u32[]{:S(2)}) %collective-permute-start.21) | collective-permute-done | bytes 262176 | tf_op jit(solution)/shard_map/ppermute | solution.py:327
  106.2 7.3 %collective-permute-start.9 = (bf16[16,64,128]{2,1,0:T(8,128)(2,1)}, bf16[16,64,128]{2,1,0:T(8,128)(2,1)}, u32[]{:S(2)}, u32[]{:S(2)}) collective-permute-start(bf16[16,64,128]{2,1,0:T(8,128)(2,1)} %get-tuple-element.100), channel_id=1, source_target_pairs={{0,4},{1,5},{2,6},{3,7},{4,0},{5,1},{6,2},{7,3},{8,12},{9,13},{10,... | collective-permute-start | bytes 786440 | tf_op jit(solution)/shard_map/ppermute | solution.py:327
  114.9 2.0 %collective-permute-done.7 = bf16[16,64,128]{2,1,0:T(8,128)(2,1)} collective-permute-done((bf16[16,64,128]{2,1,0:T(8,128)(2,1)}, bf16[16,64,128]{2,1,0:T(8,128)(2,1)}, u32[]{:S(2)}, u32[]{:S(2)}) %collective-permute-start.7) | collective-permute-done | bytes 262176 | tf_op jit(solution)/shard_map/ppermute | solution.py:327
  116.9 2.1 %collective-permute-start.12 = (bf16[16,64,128]{2,1,0:T(8,128)(2,1)}, bf16[16,64,128]{2,1,0:T(8,128)(2,1)}, u32[]{:S(2)}, u32[]{:S(2)}) collective-permute-start(bf16[16,64,128]{2,1,0:T(8,128)(2,1)} %get-tuple-element.103), channel_id=1, source_target_pairs={{0,7},{1,6},{2,5},{3,4},{4,3},{5,2},{6,1},{7,0},{8,15},{9,14},{10,... | collective-permute-start | bytes 786440 | tf_op jit(solution)/shard_map/ppermute | solution.py:327
  119.0 3.3 %all-to-all-start = ((s32[8,1,128]{2,1,0:T(1,128)}), s32[8,1,128]{2,1,0:T(1,128)S(1)}, u32[]{:S(2)}, u32[]{:S(2)}) async-start(s32[8,1,128]{2,1,0:T(1,128)} %bitcast.12), calls=%async_computation.1 | async-start | bytes 8192 | tf_op jit(solution)/shard_map/all_to_all | solution.py:280
  122.4 47.3 %pmax.7 = s32[]{:T(128)} all-reduce(s32[]{:T(128)} %bitcast.10), channel_id=1, replica_groups=mesh['row'=4,'col'=8] {'row','col'}, use_global_device_ids=true, to_apply=%region_0.0 | all-reduce | flops 1 | bytes 8 | tf_op jit(solution)/shard_map/pmax | solution.py:358
  170.3 3.5 %combine.3 = bf16[128,8192]{1,0:T(8,128)(2,1)} custom-call(s32[8,128]{1,0:T(8,128)S(1)} %bitcast.59, bf16[128,8192]{1,0:T(8,128)(2,1)S(1)} %copy-done, bf16[64,64,128]{2,1,0:T(8,128)(2,1)} %get-tuple-element.108.refs_2_, bf16[16,64,128]{2,1,0:T(8,128)(2,1)} %copy-done.7, bf16[16,64,128]{2,1,0:T(8,128)(2,1)} %copy-done.8, ...), custom_call_target="tpu_custom_call" | custom-call | flops 2097152 | bytes 4980736 | tf_op jit(solution)/shard_map/combine/pallas_call | solution.py:332
  173.9 3.2 %conditional.1 = (bf16[128,8192]{1,0:T(8,128)(2,1)}) conditional(s32[]{:T(128)} %convert_element_type.15, (s32[8,128]{1,0:T(8,128)S(1)}, bf16[128,8192]{1,0:T(8,128)(2,1)S(1)}, bf16[64,64,128]{2,1,0:T(8,128)(2,1)S(1)}, bf16[16,64,128]{2,1,0:T(8,128)(2,1)S(1)}, bf16[16,64,128]{2,1,0:T(8,128)(2,1)}, /*index=5*/bf16[16,64,128]{2,1,0:T(8,128)(2,1)}, ...), branch_computations={%region_1.0_spmd, %region_2.5_spmd} | conditional | flops 285219200 | bytes 262150464 | solution.py:359
  173.9 3.1 %combine.2 = bf16[128,8192]{1,0:T(8,128)(2,1)} custom-call(s32[8,128]{1,0:T(8,128)S(1)} %get-tuple-element.36.refs_0_, bf16[128,8192]{1,0:T(8,128)(2,1)S(1)} %get-tuple-element.37.refs_1_, bf16[64,64,128]{2,1,0:T(8,128)(2,1)S(1)} %get-tuple-element.38.refs_2_, bf16[16,64,128]{2,1,0:T(8,128)(2,1)S(1)} %get-tuple-element.39.refs_3_, ...), custom_call_target="tpu_custom_call", output_to_operand_aliasing={{}: (10, {})} | custom-call | flops 2097152 | bytes 4980736 | tf_op jit(solution)/shard_map/cond/branch_0_fun/combine/pallas_call | solution.py:332
  (64 shorter events, 12.3 us)
Async XLA Ops:
  9.6 5.9 %collective-permute-start = (s32[1,128]{1,0:T(1,128)}, s32[1,128]{1,0:T(1,128)S(1)}, u32[]{:S(2)}, u32[]{:S(2)}) collective-permute-start(s32[1,128]{1,0:T(1,128)} %get-tuple-element.89), channel_id=1, source_target_pairs={{0,8},{8,0},{16,24},{24,16},{1,9},{9,1},{17,25},{25,17},{2,10},{10... | collective-permute-start | bytes 1544 | tf_op jit(solution)/shard_map/ppermute | solution.py:262
  12.6 4.7 %collective-permute-start.1 = (s32[1,128]{1,0:T(1,128)}, s32[1,128]{1,0:T(1,128)S(1)}, u32[]{:S(2)}, u32[]{:S(2)}) collective-permute-start(s32[1,128]{1,0:T(1,128)} %get-tuple-element.90), channel_id=1, source_target_pairs={{0,16},{8,24},{16,0},{24,8},{1,17},{9,25},{17,1},{25,9},{2,18},{10... | collective-permute-start | bytes 1544 | tf_op jit(solution)/shard_map/ppermute | solution.py:262
  15.4 5.5 %collective-permute-start.2 = (s32[1,128]{1,0:T(1,128)}, s32[1,128]{1,0:T(1,128)S(1)}, u32[]{:S(2)}, u32[]{:S(2)}) collective-permute-start(s32[1,128]{1,0:T(1,128)} %get-tuple-element.91), channel_id=1, source_target_pairs={{0,24},{8,16},{16,8},{24,0},{1,25},{9,17},{17,9},{25,1},{2,26},{10... | collective-permute-start | bytes 1544 | tf_op jit(solution)/shard_map/ppermute | solution.py:262
  24.6 18.7 %collective-permute-start.13 = (bf16[24,64,128]{2,1,0:T(8,128)(2,1)}, bf16[24,64,128]{2,1,0:T(8,128)(2,1)S(1)}, u32[]{:S(2)}, u32[]{:S(2)}) collective-permute-start(bf16[24,64,128]{2,1,0:T(8,128)(2,1)} %get-tuple-element.105), channel_id=1, source_target_pairs={{0,8},{8,0},{16,24},{24,16},{1,9},{9,1},{17,25},{25,17},{2,10},{10... | collective-permute-start | bytes 1179656 | tf_op jit(solution)/shard_map/ppermute | solution.py:301
  24.6 30.2 %collective-permute-start.14 = (bf16[24,64,128]{2,1,0:T(8,128)(2,1)}, bf16[24,64,128]{2,1,0:T(8,128)(2,1)}, u32[]{:S(2)}, u32[]{:S(2)}) collective-permute-start(bf16[24,64,128]{2,1,0:T(8,128)(2,1)} %get-tuple-element.106), channel_id=1, source_target_pairs={{0,16},{8,24},{16,0},{24,8},{1,17},{9,25},{17,1},{25,9},{2,18},{10... | collective-permute-start | bytes 1179656 | tf_op jit(solution)/shard_map/ppermute | solution.py:301
  25.0 29.7 %collective-permute-start.15 = (bf16[24,64,128]{2,1,0:T(8,128)(2,1)}, bf16[24,64,128]{2,1,0:T(8,128)(2,1)}, u32[]{:S(2)}, u32[]{:S(2)}) collective-permute-start(bf16[24,64,128]{2,1,0:T(8,128)(2,1)} %get-tuple-element.107), channel_id=1, source_target_pairs={{0,24},{8,16},{16,8},{24,0},{1,25},{9,17},{17,9},{25,1},{2,26},{10... | collective-permute-start | bytes 1179656 | tf_op jit(solution)/shard_map/ppermute | solution.py:301
  31.4 30.7 %collective-permute-start.3 = (bf16[24,64,128]{2,1,0:T(8,128)(2,1)}, bf16[24,64,128]{2,1,0:T(8,128)(2,1)S(1)}, u32[]{:S(2)}, u32[]{:S(2)}) collective-permute-start(bf16[24,64,128]{2,1,0:T(8,128)(2,1)} %get-tuple-element.93), channel_id=1, source_target_pairs={{0,8},{8,0},{16,24},{24,16},{1,9},{9,1},{17,25},{25,17},{2,10},{10... | collective-permute-start | bytes 1179656 | tf_op jit(solution)/shard_map/ppermute | solution.py:301
  31.4 57.0 %collective-permute-start.4 = (bf16[24,64,128]{2,1,0:T(8,128)(2,1)}, bf16[24,64,128]{2,1,0:T(8,128)(2,1)S(1)}, u32[]{:S(2)}, u32[]{:S(2)}) collective-permute-start(bf16[24,64,128]{2,1,0:T(8,128)(2,1)} %get-tuple-element.94), channel_id=1, source_target_pairs={{0,16},{8,24},{16,0},{24,8},{1,17},{9,25},{17,1},{25,9},{2,18},{10... | collective-permute-start | bytes 1179656 | tf_op jit(solution)/shard_map/ppermute | solution.py:301
  44.0 45.5 %collective-permute-start.5 = (bf16[24,64,128]{2,1,0:T(8,128)(2,1)}, bf16[24,64,128]{2,1,0:T(8,128)(2,1)S(1)}, u32[]{:S(2)}, u32[]{:S(2)}) collective-permute-start(bf16[24,64,128]{2,1,0:T(8,128)(2,1)} %get-tuple-element.95), channel_id=1, source_target_pairs={{0,24},{8,16},{16,8},{24,0},{1,25},{9,17},{17,9},{25,1},{2,26},{10... | collective-permute-start | bytes 1179656 | tf_op jit(solution)/shard_map/ppermute | solution.py:301
  60.7 35.2 %collective-permute-start.16 = (bf16[16,64,128]{2,1,0:T(8,128)(2,1)}, bf16[16,64,128]{2,1,0:T(8,128)(2,1)S(1)}, u32[]{:S(2)}, u32[]{:S(2)}) collective-permute-start(bf16[16,64,128]{2,1,0:T(8,128)(2,1)} %get-tuple-element.109), channel_id=1, source_target_pairs={{0,1},{1,0},{2,3},{3,2},{4,5},{5,4},{6,7},{7,6},{8,9},{9,8},{10,11... | collective-permute-start | bytes 786440 | tf_op jit(solution)/shard_map/ppermute | solution.py:327
  60.8 36.9 %collective-permute-start.17 = (bf16[16,64,128]{2,1,0:T(8,128)(2,1)}, bf16[16,64,128]{2,1,0:T(8,128)(2,1)S(1)}, u32[]{:S(2)}, u32[]{:S(2)}) collective-permute-start(bf16[16,64,128]{2,1,0:T(8,128)(2,1)} %get-tuple-element.110), channel_id=1, source_target_pairs={{0,2},{1,3},{2,0},{3,1},{4,6},{5,7},{6,4},{7,5},{8,10},{9,11},{10,... | collective-permute-start | bytes 786440 | tf_op jit(solution)/shard_map/ppermute | solution.py:327
  62.1 37.2 %collective-permute-start.18 = (bf16[16,64,128]{2,1,0:T(8,128)(2,1)}, bf16[16,64,128]{2,1,0:T(8,128)(2,1)}, u32[]{:S(2)}, u32[]{:S(2)}) collective-permute-start(bf16[16,64,128]{2,1,0:T(8,128)(2,1)} %get-tuple-element.111), channel_id=1, source_target_pairs={{0,3},{1,2},{2,1},{3,0},{4,7},{5,6},{6,5},{7,4},{8,11},{9,10},{10,... | collective-permute-start | bytes 786440 | tf_op jit(solution)/shard_map/ppermute | solution.py:327
  88.3 11.1 %collective-permute-start.19 = (bf16[16,64,128]{2,1,0:T(8,128)(2,1)}, bf16[16,64,128]{2,1,0:T(8,128)(2,1)}, u32[]{:S(2)}, u32[]{:S(2)}) collective-permute-start(bf16[16,64,128]{2,1,0:T(8,128)(2,1)} %get-tuple-element.112), channel_id=1, source_target_pairs={{0,4},{1,5},{2,6},{3,7},{4,0},{5,1},{6,2},{7,3},{8,12},{9,13},{10,... | collective-permute-start | bytes 786440 | tf_op jit(solution)/shard_map/ppermute | solution.py:327
  89.5 11.5 %collective-permute-start.20 = (bf16[16,64,128]{2,1,0:T(8,128)(2,1)}, bf16[16,64,128]{2,1,0:T(8,128)(2,1)}, u32[]{:S(2)}, u32[]{:S(2)}) collective-permute-start(bf16[16,64,128]{2,1,0:T(8,128)(2,1)} %get-tuple-element.113), channel_id=1, source_target_pairs={{0,5},{1,4},{2,7},{3,6},{4,1},{5,0},{6,3},{7,2},{8,13},{9,12},{10,... | collective-permute-start | bytes 786440 | tf_op jit(solution)/shard_map/ppermute | solution.py:327
  95.9 10.3 %collective-permute-start.21 = (bf16[16,64,128]{2,1,0:T(8,128)(2,1)}, bf16[16,64,128]{2,1,0:T(8,128)(2,1)S(1)}, u32[]{:S(2)}, u32[]{:S(2)}) collective-permute-start(bf16[16,64,128]{2,1,0:T(8,128)(2,1)} %get-tuple-element.114), channel_id=1, source_target_pairs={{0,6},{1,7},{2,4},{3,5},{4,2},{5,3},{6,0},{7,1},{8,14},{9,15},{10,... | collective-permute-start | bytes 786440 | tf_op jit(solution)/shard_map/ppermute | solution.py:327
  97.7 15.8 %collective-permute-start.22 = (bf16[16,64,128]{2,1,0:T(8,128)(2,1)}, bf16[16,64,128]{2,1,0:T(8,128)(2,1)S(1)}, u32[]{:S(2)}, u32[]{:S(2)}) collective-permute-start(bf16[16,64,128]{2,1,0:T(8,128)(2,1)} %get-tuple-element.115), channel_id=1, source_target_pairs={{0,7},{1,6},{2,5},{3,4},{4,3},{5,2},{6,1},{7,0},{8,15},{9,14},{10,... | collective-permute-start | bytes 786440 | tf_op jit(solution)/shard_map/ppermute | solution.py:327
  99.3 14.2 %collective-permute-start.6 = (bf16[16,64,128]{2,1,0:T(8,128)(2,1)}, bf16[16,64,128]{2,1,0:T(8,128)(2,1)S(1)}, u32[]{:S(2)}, u32[]{:S(2)}) collective-permute-start(bf16[16,64,128]{2,1,0:T(8,128)(2,1)} %get-tuple-element.97), channel_id=1, source_target_pairs={{0,1},{1,0},{2,3},{3,2},{4,5},{5,4},{6,7},{7,6},{8,9},{9,8},{10,11... | collective-permute-start | bytes 786440 | tf_op jit(solution)/shard_map/ppermute | solution.py:327
  99.4 17.5 %collective-permute-start.7 = (bf16[16,64,128]{2,1,0:T(8,128)(2,1)}, bf16[16,64,128]{2,1,0:T(8,128)(2,1)}, u32[]{:S(2)}, u32[]{:S(2)}) collective-permute-start(bf16[16,64,128]{2,1,0:T(8,128)(2,1)} %get-tuple-element.98), channel_id=1, source_target_pairs={{0,2},{1,3},{2,0},{3,1},{4,6},{5,7},{6,4},{7,5},{8,10},{9,11},{10,... | collective-permute-start | bytes 786440 | tf_op jit(solution)/shard_map/ppermute | solution.py:327
  101.0 72.9 %collective-permute-start.8 = (bf16[16,64,128]{2,1,0:T(8,128)(2,1)}, bf16[16,64,128]{2,1,0:T(8,128)(2,1)}, u32[]{:S(2)}, u32[]{:S(2)}) collective-permute-start(bf16[16,64,128]{2,1,0:T(8,128)(2,1)} %get-tuple-element.99), channel_id=1, source_target_pairs={{0,3},{1,2},{2,1},{3,0},{4,7},{5,6},{6,5},{7,4},{8,11},{9,10},{10,... | collective-permute-start | bytes 786440 | tf_op jit(solution)/shard_map/ppermute | solution.py:327
  106.2 67.7 %collective-permute-start.9 = (bf16[16,64,128]{2,1,0:T(8,128)(2,1)}, bf16[16,64,128]{2,1,0:T(8,128)(2,1)}, u32[]{:S(2)}, u32[]{:S(2)}) collective-permute-start(bf16[16,64,128]{2,1,0:T(8,128)(2,1)} %get-tuple-element.100), channel_id=1, source_target_pairs={{0,4},{1,5},{2,6},{3,7},{4,0},{5,1},{6,2},{7,3},{8,12},{9,13},{10,... | collective-permute-start | bytes 786440 | tf_op jit(solution)/shard_map/ppermute | solution.py:327
  113.5 60.3 %collective-permute-start.10 = (bf16[16,64,128]{2,1,0:T(8,128)(2,1)}, bf16[16,64,128]{2,1,0:T(8,128)(2,1)}, u32[]{:S(2)}, u32[]{:S(2)}) collective-permute-start(bf16[16,64,128]{2,1,0:T(8,128)(2,1)} %get-tuple-element.101), channel_id=1, source_target_pairs={{0,5},{1,4},{2,7},{3,6},{4,1},{5,0},{6,3},{7,2},{8,13},{9,12},{10,... | collective-permute-start | bytes 786440 | tf_op jit(solution)/shard_map/ppermute | solution.py:327
  113.6 60.3 %collective-permute-start.11 = (bf16[16,64,128]{2,1,0:T(8,128)(2,1)}, bf16[16,64,128]{2,1,0:T(8,128)(2,1)}, u32[]{:S(2)}, u32[]{:S(2)}) collective-permute-start(bf16[16,64,128]{2,1,0:T(8,128)(2,1)} %get-tuple-element.102), channel_id=1, source_target_pairs={{0,6},{1,7},{2,4},{3,5},{4,2},{5,3},{6,0},{7,1},{8,14},{9,15},{10,... | collective-permute-start | bytes 786440 | tf_op jit(solution)/shard_map/ppermute | solution.py:327
  116.9 57.0 %collective-permute-start.12 = (bf16[16,64,128]{2,1,0:T(8,128)(2,1)}, bf16[16,64,128]{2,1,0:T(8,128)(2,1)}, u32[]{:S(2)}, u32[]{:S(2)}) collective-permute-start(bf16[16,64,128]{2,1,0:T(8,128)(2,1)} %get-tuple-element.103), channel_id=1, source_target_pairs={{0,7},{1,6},{2,5},{3,4},{4,3},{5,2},{6,1},{7,0},{8,15},{9,14},{10,... | collective-permute-start | bytes 786440 | tf_op jit(solution)/shard_map/ppermute | solution.py:327
  119.0 51.4 %all-to-all-start = ((s32[8,1,128]{2,1,0:T(1,128)}), s32[8,1,128]{2,1,0:T(1,128)S(1)}, u32[]{:S(2)}, u32[]{:S(2)}) async-start(s32[8,1,128]{2,1,0:T(1,128)} %bitcast.12), calls=%async_computation.1 | async-start | bytes 8192 | tf_op jit(solution)/shard_map/all_to_all | solution.py:280
  (15 other events, 196.5 us)

commit v2 on v0

v2 whole, which is shorter than its diff:
```python
import jax
import jax.numpy as jnp
from jax import lax
from jax.experimental import pallas as pl
from jax.experimental.pallas import tpu as pltpu
from jax.sharding import PartitionSpec as P

CAP_ROW = 24
CAP_COL = 16
PARTS = 2
VMEM_LIMIT = 60 * 1024 * 1024


def smem():
    return pl.BlockSpec(memory_space=pltpu.SMEM)


def anywhere():
    return pl.BlockSpec(memory_space=pl.ANY)


def one(shape, at=None):
    at = (0,) * len(shape) if at is None else at
    return pl.BlockSpec(shape, lambda i: at)


def number(index, per_piece, owner_of, n_owner, cap, wide):
    slots = index.shape[1]
    f32 = jnp.float32
    lane = lax.broadcasted_iota(jnp.int32, (slots, slots), 1)
    sub = lax.broadcasted_iota(jnp.int32, (slots, slots), 0)
    key_r = index.astype(f32)
    key_c = jnp.sum(jnp.where(lane == sub, key_r, 0.0), axis=1, keepdims=True)
    index_c = key_c.astype(jnp.int32)

    def split(values):
        return owner_of(jnp.maximum(values, 0)).astype(f32), lax.rem(jnp.maximum(values, 0), per_piece).astype(f32)

    owner_r, _ = split(index)
    owner_c, local_c = split(index_c)
    same = jnp.where(key_c == key_r, 1.0, 0.0)
    before = jnp.where(lane < sub, 1.0, 0.0)
    after = jnp.where(sub < lane, 1.0, 0.0)
    kin = jnp.where(owner_c == owner_r, 1.0, 0.0)
    first_c = jnp.where(jnp.sum(same * before, axis=1, keepdims=True) == 0.0, 1.0, 0.0)
    first_c = jnp.where(key_c >= 0.0, first_c, 0.0)
    first_r = jnp.where(jnp.sum(same * after, axis=0, keepdims=True) == 0.0, 1.0, 0.0)
    first_r = jnp.where(key_r >= 0.0, first_r, 0.0)
    rank_c = jnp.sum(kin * before * first_r, axis=1, keepdims=True)
    at_r = jnp.sum(same * (first_c * rank_c), axis=0, keepdims=True)
    place = owner_r * cap + jnp.minimum(at_r, cap - 1.0)
    wide_lane = lax.broadcasted_iota(jnp.int32, (slots, wide), 1).astype(f32)
    spot = jnp.where(wide_lane == rank_c + 1.0, local_c, 0.0) + jnp.where(wide_lane == 0.0, 1.0, 0.0)
    rows = []
    for owner in range(n_owner):
        mine = first_c * jnp.where(owner_c == float(owner), 1.0, 0.0)
        rows.append(jnp.sum(spot * mine, axis=0, keepdims=True))
    return place, first_r, rows


def ask_kernel(n_row, n_col, per_piece, cap_row, cap_col, index, asks, lists, places):
    wide = asks.shape[1]
    k, j = index[0, 0, 0:1, :], index[0, 0, 1:2, :]
    place_in, _, ask_rows = number(
        k, per_piece, lambda v: lax.div(v, per_piece * n_col), n_row, cap_row, wide
    )
    place_out, first, list_rows = number(
        j, per_piece, lambda v: lax.rem(lax.div(v, per_piece), n_col), n_col, cap_col, wide
    )
    excess = jnp.full((1, 1), -1.0, jnp.float32)
    for cap, rows in ((cap_row, ask_rows), (cap_col, list_rows)):
        for row in rows:
            excess = jnp.maximum(excess, row[:, 0:1] - float(cap))
    lane = lax.broadcasted_iota(jnp.int32, (1, wide), 1)
    for i, row in enumerate(ask_rows):
        asks[i : i + 1, :] = jnp.where(lane == wide - 1, excess, row).astype(jnp.int32)
    for i, row in enumerate(list_rows):
        lists[i : i + 1, :] = row.astype(jnp.int32)
    alive = jnp.where(j >= 0, 1.0, 0.0)
    places[0:1, :] = place_in.astype(jnp.int32)
    places[1:2, :] = jnp.where(j >= 0, place_out, float(n_col * cap_col)).astype(jnp.int32)
    places[2:3, :] = first.astype(jnp.int32)
    live = jnp.sum(alive, axis=1, keepdims=True)
    places[3:4, :] = jnp.broadcast_to(live, j.shape).astype(jnp.int32)


def pack_kernel(blk, asks, slab, packs):
    n_row, cap = packs.shape[:2]
    for t in range(n_row):

        def copy(i, carry):
            at = pl.multiple_of(asks[t, 1 + i] * blk, blk)
            packs[t, i] = slab[:, pl.ds(at, blk)]
            return carry

        lax.fori_loop(0, jnp.minimum(asks[t, 0], cap), copy, 0)


def product_kernel(group, places, lists, stored, panels, sums, total):
    n_col, cap = sums.shape[:2]
    slots = places.shape[1]
    live = places[3, 0]

    def step(g, carry):
        products = []
        for u in range(group):
            s = g * group + u
            products.append(
                jnp.dot(panels[places[0, s]], stored[s], preferred_element_type=jnp.float32)
            )
        for u in range(group):
            s = g * group + u
            o = places[1, s]
            total[o] = jnp.where(places[2, s] == 1, 0.0, total[o]) + products[u]
        return carry

    lax.fori_loop(0, lax.div(live + group - 1, group), step, 0)
    for t in range(n_col):

        def store(i, carry):
            sums[t, i] = total[t * cap + i].astype(jnp.bfloat16)
            return carry

        lax.fori_loop(0, jnp.minimum(lists[t, 0], cap), store, 0)


def combine_kernel(blk, lists, slab, sums, *refs):
    out, total = refs[-2], refs[-1]
    n_col, cap = sums.shape[:2]
    total[...] = jnp.zeros_like(total)
    for t in range(n_col):

        def add(i, carry):
            total[lists[t, 1 + i]] += sums[t, i].astype(jnp.float32)
            return carry

        lax.fori_loop(0, jnp.minimum(lists[t, 0], cap), add, 0)
    for i in range(out.shape[1] // blk):
        here = pl.ds(i * blk, blk)
        out[:, here] = (3.0 * slab[:, here].astype(jnp.float32) - 2.0 * total[i]).astype(out.dtype)


def dense(s_slab, p_blocks, p_index):
    blk = s_slab.shape[0]
    per_piece = s_slab.shape[1] // blk
    n_row = lax.axis_size("row")
    n_col = lax.axis_size("col")
    span = n_col * per_piece
    gathered = lax.all_gather(s_slab, "row", axis=1, tiled=True)
    panels = gathered.reshape(blk, n_row * per_piece, blk)
    block_rows = p_index[0, 0, 0]
    block_cols = p_index[0, 0, 1]
    local_rows = jnp.clip(
        block_rows // per_piece // n_col * per_piece + block_rows % per_piece,
        0,
        n_row * per_piece - 1,
    )
    local_cols = jnp.where(block_cols >= 0, block_cols - lax.axis_index("row") * span, span)
    taken = jnp.take(panels, local_rows, axis=1)
    product = jnp.einsum("agk,gkb->gab", taken, p_blocks[0, 0], preferred_element_type=jnp.float32)
    term = jax.ops.segment_sum(product, local_cols, num_segments=span)
    cube = lax.psum_scatter(term.astype(jnp.bfloat16), "col", scatter_dimension=0, tiled=True)
    cube = cube.astype(jnp.float32).transpose(1, 0, 2).reshape(blk, per_piece * blk)
    return (3.0 * s_slab.astype(jnp.float32) - 2.0 * cube).astype(jnp.bfloat16)


def body(s_slab, p_blocks, p_index):
    blk = s_slab.shape[0]
    per_piece = s_slab.shape[1] // blk
    n_row = lax.axis_size("row")
    n_col = lax.axis_size("col")
    slots = p_blocks.shape[2]
    stored = p_blocks[0, 0]
    full = min(per_piece, slots)
    cap_row = min(CAP_ROW, full)
    cap_col = min(CAP_COL, full)
    wide = -(-(2 + full) // 128) * 128
    parts = PARTS if blk % (16 * PARTS) == 0 else 1
    rows = blk // parts
    group = 4 if slots % 4 == 0 else 1
    params = pltpu.CompilerParams(vmem_limit_bytes=VMEM_LIMIT)

    asks, lists, places = pl.pallas_call(
        lambda *refs: ask_kernel(n_row, n_col, per_piece, cap_row, cap_col, *refs),
        out_shape=[
            jax.ShapeDtypeStruct((n_row, wide), jnp.int32),
            jax.ShapeDtypeStruct((n_col, wide), jnp.int32),
            jax.ShapeDtypeStruct((4, slots), jnp.int32),
        ],
        compiler_params=params,
        name="ask",
    )(p_index)
    asked = lax.all_to_all(asks, "row", 0, 0, tiled=True)

    packed = [
        pl.pallas_call(
            lambda *refs: pack_kernel(blk, *refs),
            grid=(1,),
            out_shape=jax.ShapeDtypeStruct((n_row, cap_row, rows, blk), jnp.bfloat16),
            in_specs=[smem(), one((rows, s_slab.shape[1]), (part, 0))],
            out_specs=one((n_row, cap_row, rows, blk)),
            compiler_params=params,
            cost_estimate=pl.CostEstimate(
                flops=0, bytes_accessed=4 * s_slab.size // parts, transcendentals=0
            ),
            name="pack",
        )(asked, s_slab)
        for part in range(parts)
    ]
    fetched = [lax.all_to_all(part, "row", 0, 0, tiled=True) for part in packed]

    worst = jnp.max(asked[:, wide - 1])
    told = jnp.where(jnp.arange(wide)[None] == wide - 1, worst, lists)
    told = lax.all_to_all(told, "col", 0, 0, tiled=True)

    sums = []
    for part in range(parts):
        done = pl.pallas_call(
            lambda *refs: product_kernel(group, *refs),
            grid=(1,),
            out_shape=jax.ShapeDtypeStruct((n_col, cap_col, rows, blk), jnp.bfloat16),
            in_specs=[smem()] * 2
            + [one(stored.shape), one((n_row * cap_row, rows, blk))],
            out_specs=one((n_col, cap_col, rows, blk)),
            scratch_shapes=[pltpu.VMEM((n_col * cap_col + 1, rows, blk), jnp.float32)],
            compiler_params=params,
            cost_estimate=pl.CostEstimate(
                flops=2 * slots * rows * blk * blk,
                bytes_accessed=2 * blk * blk * slots
                + 2 * rows * blk * (n_row * cap_row + n_col * cap_col),
                transcendentals=0,
            ),
            name="product",
        )(places, lists, stored, fetched[part].reshape(n_row * cap_row, rows, blk))
        sums.append(lax.all_to_all(done, "col", 0, 0, tiled=True))

    def combine(part, before):
        extra = [] if before is None else [before]
        return pl.pallas_call(
            lambda *refs: combine_kernel(blk, *refs),
            grid=(1,),
            out_shape=jax.ShapeDtypeStruct(s_slab.shape, s_slab.dtype),
            in_specs=[
                smem(),
                one((rows, s_slab.shape[1]), (part, 0)),
                one((n_col, cap_col, rows, blk)),
            ]
            + [anywhere()] * len(extra),
            out_specs=one((rows, s_slab.shape[1]), (part, 0)),
            scratch_shapes=[pltpu.VMEM((per_piece, rows, blk), jnp.float32)],
            input_output_aliases={3: 0} if extra else {},
            compiler_params=params,
            cost_estimate=pl.CostEstimate(
                flops=4 * s_slab.size // parts,
                bytes_accessed=4 * s_slab.size // parts + 2 * rows * blk * n_col * cap_col,
                transcendentals=0,
            ),
            name="combine",
        )(told, s_slab, sums[part], *extra)

    result = None
    for part in range(parts - 1):
        result = combine(part, result)
    if cap_row == full and cap_col == full:
        return combine(parts - 1, result)
    return lax.cond(
        jnp.max(told[:, wide - 1]) > 0,
        lambda: dense(s_slab, p_blocks, p_index),
        lambda: combine(parts - 1, result),
    )


def solution(mesh):
    placed = (
        P(None, ("row", "col")),
        P("row", "col", None, None, None),
        P("row", "col", None, None),
    )
    return jax.shard_map(
        body, mesh=mesh, in_specs=placed, out_specs=P(None, ("row", "col")), check_vma=False
    )
```

time: 368 us -> 186 us (0.51)
  waiting for transfers between devices: 267 us -> 116 us
  local copies, waits for them, and re-layouts: 42.6 us -> 0.01 us
  other arithmetic: 39.9 us -> 3.32 us
  starting transfers between devices: 0.04 us -> 27.4 us
  Pallas kernels: 0 us -> 25 us
  matrix products: 4.41 us -> 0 us
    all_gather x1 -> x0, waiting for transfers between devices: 152 us -> none  [body(): gathered = lax.all_gather(s_slab, 'row', axis=1, tiled=True)]
    all_to_all x0 -> x6, waiting for transfers between devices: none -> 116 us  [the longest x2 65.7 us: body(): fetched = [lax.all_to_all(part, 'row', 0, 0, tiled=True) for part in packed]]
    reduce_scatter x1 -> x0, waiting for transfers between devices: 115 us -> none  [body(): lax.psum_scatter(lax.fori_loop(0, slots // group, add_group, start).astyp...]
    all_to_all x0 -> x6, starting transfers between devices: none -> 27.4 us  [the longest x2 8.7 us: body(): fetched = [lax.all_to_all(part, 'row', 0, 0, tiled=True) for part in packed]]
    pallas_call x0 -> x7, Pallas kernels: none -> 25 us  [the longest x2 11.8 us: body(): pl.pallas_call(lambda *refs: product_kernel(group, *refs), grid=(1,), out...]
    convert_element_type x2 -> x0, other arithmetic: 22.6 us -> none  [the longest x1 17.7 us: body(): lax.fori_loop(0, slots // group, add_group, start).astype(jnp.bfloat16)]
    scatter-add x1 -> x0, other arithmetic: 13.1 us -> none  [add_group(): return total + jax.ops.segment_sum(product, target, num_segments=span)]
    reshape x1 -> x0, local copies, waits for them, and re-layouts: 12 us -> none  [body(): panels = gathered.reshape(blk, n_row * per_piece, blk)]
  transfers between devices with their start and end apart: 2 -> 6, of which waited for: 2 -> 6; matrix products, arithmetic and copies ran while one was open for 0% -> 0% of each run, Pallas kernels for 0% -> 11%
where the time goes in v2:
time: 186 us
  waiting for transfers between devices  116 us (62%)
  starting transfers between devices  27.4 us (15%)
  Pallas kernels  25 us (13%)
  between operations  14.1 us (8%)
  other arithmetic  3.32 us (2%)
    all_to_all x2, waiting for transfers between devices, body(): fetched = [lax.all_to_all(part, 'row', 0, 0, tiled=True) for part in packed]  65.7 us
    all_to_all x2, waiting for transfers between devices, body(): sums.append(lax.all_to_all(done, 'col', 0, 0, tiled=True))  42.7 us
    pallas_call x2, Pallas kernels, body(): pl.pallas_call(lambda *refs: product_kernel(group, *refs), grid=(1,), out...  11.8 us
    all_to_all x2, starting transfers between devices, body(): fetched = [lax.all_to_all(part, 'row', 0, 0, tiled=True) for part in packed]  8.7 us
    all_to_all x2, starting transfers between devices, body(): sums.append(lax.all_to_all(done, 'col', 0, 0, tiled=True))  8.68 us
    pallas_call x2, Pallas kernels, combine(): pl.pallas_call(lambda *refs: combine_kernel(blk, *refs), grid=(1,), out_s...  6.65 us
    all_to_all x1, starting transfers between devices, body(): asked = lax.all_to_all(asks, 'row', 0, 0, tiled=True)  6.32 us
    all_to_all x1, waiting for transfers between devices, body(): asked = lax.all_to_all(asks, 'row', 0, 0, tiled=True)  5.46 us
  transfers between devices with their start and end apart: 6, of which 6 were waited for; matrix products, arithmetic and copies ran while one was open for 0% of the time, Pallas kernels for 11%

profile of v2, /device:TPU:0, one launch (start us, length us, event | category | flops | bytes accessed | tf_op | source)
XLA Modules:
  0.0 185.6 jit_solution(9502615566605637016)
XLA Ops:
  6.5 1.6 ask.1
  8.1 6.3 %all-to-all-start = ((s32[4,1,128]{2,1,0:T(1,128)}), s32[4,1,128]{2,1,0:T(1,128)S(1)}, u32[]{:S(2)}, u32[]{:S(2)}) async-start(s32[4,1,128]{2,1,0:T(1,128)} %bitcast.67), calls=%async_computation.1 | async-start | bytes 4096 | tf_op jit(solution)/shard_map/all_to_all | solution.py:193
  14.5 5.5 %all-to-all-done = s32[4,1,128]{2,1,0:T(1,128)S(1)} async-done(((s32[4,1,128]{2,1,0:T(1,128)}), s32[4,1,128]{2,1,0:T(1,128)S(1)}, u32[]{:S(2)}, u32[]{:S(2)}) %all-to-all-start) | async-done | bytes 2080 | tf_op jit(solution)/shard_map/all_to_all | solution.py:193
  19.9 0.7 slice_reduce_fusion.1
  20.6 1.9 %broadcast_select_fusion = s32[8,128]{1,0:T(8,128)} fusion(s32[8,128]{1,0:T(8,128)} %get-tuple-element.33.refs_1_, s32[]{:T(128)} %slice_reduce_fusion.1, pred[128]{0:T(512)(128)(4,1)S(1)} %iota_compare_fusion), kind=kLoop, calls=%fused_computation.42 | loop fusion | flops 1024 | bytes 8324 | tf_op jit(solution)/shard_map/jit(_where)/select_n | solution.py:213
  22.6 3.7 %all-to-all-start.1 = ((s32[8,1,128]{2,1,0:T(1,128)}), s32[8,1,128]{2,1,0:T(1,128)S(1)}, u32[]{:S(2)}, u32[]{:S(2)}) async-start(s32[8,1,128]{2,1,0:T(1,128)} %bitcast.13), calls=%async_computation.2 | async-start | bytes 8192 | tf_op jit(solution)/shard_map/all_to_all | solution.py:214
  26.3 2.7 %pack.3 = bf16[4,24,64,128]{3,2,1,0:T(8,128)(2,1)} custom-call(s32[4,128]{1,0:T(4,128)} %bitcast.65, bf16[128,8192]{1,0:T(8,128)(2,1)} %refs_1_.5), custom_call_target="tpu_custom_call" | custom-call | bytes 2097152 | tf_op jit(solution)/shard_map/pack/pallas_call | solution.py:196
  29.0 1.9 %all-to-all-done.1 = s32[8,1,128]{2,1,0:T(1,128)S(1)} async-done(((s32[8,1,128]{2,1,0:T(1,128)}), s32[8,1,128]{2,1,0:T(1,128)S(1)}, u32[]{:S(2)}, u32[]{:S(2)}) %all-to-all-start.1) | async-done | bytes 4128 | tf_op jit(solution)/shard_map/all_to_all | solution.py:214
  30.9 4.3 %all-to-all-start.4 = ((bf16[4,24,64,128]{3,2,1,0:T(8,128)(2,1)}), bf16[4,24,64,128]{3,2,1,0:T(8,128)(2,1)}, u32[]{:S(2)}, u32[]{:S(2)}) async-start(bf16[4,24,64,128]{3,2,1,0:T(8,128)(2,1)} %pack.3), calls=%async_computation.5 | async-start | bytes 3145728 | tf_op jit(solution)/shard_map/all_to_all | solution.py:210
  35.3 2.1 %pack.2 = bf16[4,24,64,128]{3,2,1,0:T(8,128)(2,1)} custom-call(s32[4,128]{1,0:T(4,128)} %bitcast.66, bf16[128,8192]{1,0:T(8,128)(2,1)S(1)} %copy-done), custom_call_target="tpu_custom_call" | custom-call | bytes 2097152 | tf_op jit(solution)/shard_map/pack/pallas_call | solution.py:196
  37.4 35.1 %all-to-all-done.4 = bf16[4,24,64,128]{3,2,1,0:T(8,128)(2,1)} async-done(((bf16[4,24,64,128]{3,2,1,0:T(8,128)(2,1)}), bf16[4,24,64,128]{3,2,1,0:T(8,128)(2,1)}, u32[]{:S(2)}, u32[]{:S(2)}) %all-to-all-start.4) | async-done | bytes 1572896 | tf_op jit(solution)/shard_map/all_to_all | solution.py:210
  72.6 4.4 %all-to-all-start.2 = ((bf16[4,24,64,128]{3,2,1,0:T(8,128)(2,1)}), bf16[4,24,64,128]{3,2,1,0:T(8,128)(2,1)}, u32[]{:S(2)}, u32[]{:S(2)}) async-start(bf16[4,24,64,128]{3,2,1,0:T(8,128)(2,1)} %pack.2), calls=%async_computation.3 | async-start | bytes 3145728 | tf_op jit(solution)/shard_map/all_to_all | solution.py:210
  76.9 5.9 %product.3 = bf16[8,16,64,128]{3,2,1,0:T(8,128)(2,1)} custom-call(s32[4,64]{1,0:T(4,128)} %get-tuple-element.34.refs_0_, s32[8,128]{1,0:T(8,128)} %get-tuple-element.33.refs_1_, bf16[64,128,128]{2,1,0:T(8,128)(2,1)} %bitcast.58, bf16[96,64,128]{2,1,0:T(8,128)(2,1)} %bitcast.17.refs_3_), custom_call_target="tpu_custom_call" | custom-call | flops 134217728 | bytes 5767168 | tf_op jit(solution)/shard_map/product/pallas_call | solution.py:218
  82.8 30.6 %all-to-all-done.2 = bf16[4,24,64,128]{3,2,1,0:T(8,128)(2,1)} async-done(((bf16[4,24,64,128]{3,2,1,0:T(8,128)(2,1)}), bf16[4,24,64,128]{3,2,1,0:T(8,128)(2,1)}, u32[]{:S(2)}, u32[]{:S(2)}) %all-to-all-start.2) | async-done | bytes 1572896 | tf_op jit(solution)/shard_map/all_to_all | solution.py:210
  113.5 4.3 %all-to-all-start.5 = ((bf16[8,16,64,128]{3,2,1,0:T(8,128)(2,1)}), bf16[8,16,64,128]{3,2,1,0:T(8,128)(2,1)}, u32[]{:S(2)}, u32[]{:S(2)}) async-start(bf16[8,16,64,128]{3,2,1,0:T(8,128)(2,1)} %product.3), calls=%async_computation.6 | async-start | bytes 4194304 | tf_op jit(solution)/shard_map/all_to_all | solution.py:235
  117.8 5.9 %product.2 = bf16[8,16,64,128]{3,2,1,0:T(8,128)(2,1)} custom-call(s32[4,64]{1,0:T(4,128)} %get-tuple-element.34.refs_0_, s32[8,128]{1,0:T(8,128)} %get-tuple-element.33.refs_1_, bf16[64,128,128]{2,1,0:T(8,128)(2,1)} %bitcast.59, bf16[96,64,128]{2,1,0:T(8,128)(2,1)} %bitcast.16.refs_3_), custom_call_target="tpu_custom_call" | custom-call | flops 134217728 | bytes 5767168 | tf_op jit(solution)/shard_map/product/pallas_call | solution.py:218
  123.8 20.7 %all-to-all-done.5.refs_2_ = bf16[8,16,64,128]{3,2,1,0:T(8,128)(2,1)} async-done(((bf16[8,16,64,128]{3,2,1,0:T(8,128)(2,1)}), bf16[8,16,64,128]{3,2,1,0:T(8,128)(2,1)}, u32[]{:S(2)}, u32[]{:S(2)}) %all-to-all-start.5) | async-done | bytes 2097184 | tf_op jit(solution)/shard_map/all_to_all | solution.py:235
  144.5 4.3 %all-to-all-start.3 = ((bf16[8,16,64,128]{3,2,1,0:T(8,128)(2,1)}), bf16[8,16,64,128]{3,2,1,0:T(8,128)(2,1)}, u32[]{:S(2)}, u32[]{:S(2)}) async-start(bf16[8,16,64,128]{3,2,1,0:T(8,128)(2,1)} %product.2), calls=%async_computation.4 | async-start | bytes 4194304 | tf_op jit(solution)/shard_map/all_to_all | solution.py:235
  148.8 0.7 slice_reduce_fusion
  150.2 0.0 copy-start.4
  150.2 3.3 %combine.3 = bf16[128,8192]{1,0:T(8,128)(2,1)} custom-call(s32[8,128]{1,0:T(8,128)S(1)} %bitcast.62, bf16[128,8192]{1,0:T(8,128)(2,1)S(1)} %copy-done, bf16[8,16,64,128]{3,2,1,0:T(8,128)(2,1)} %all-to-all-done.5.refs_2_), custom_call_target="tpu_custom_call" | custom-call | flops 2097152 | bytes 4194304 | tf_op jit(solution)/shard_map/combine/pallas_call | solution.py:239
  153.5 22.0 %all-to-all-done.3 = bf16[8,16,64,128]{3,2,1,0:T(8,128)(2,1)} async-done(((bf16[8,16,64,128]{3,2,1,0:T(8,128)(2,1)}), bf16[8,16,64,128]{3,2,1,0:T(8,128)(2,1)}, u32[]{:S(2)}, u32[]{:S(2)}) %all-to-all-start.3) | async-done | bytes 2097184 | tf_op jit(solution)/shard_map/all_to_all | solution.py:235
  175.5 3.3 %conditional.1 = (bf16[128,8192]{1,0:T(8,128)(2,1)}) conditional(s32[]{:T(128)} %convert_element_type.15, (s32[8,128]{1,0:T(8,128)S(1)}, bf16[128,8192]{1,0:T(8,128)(2,1)S(1)}, bf16[8,16,64,128]{3,2,1,0:T(8,128)(2,1)}, bf16[128,8192]{1,0:T(8,128)(2,1)}) %tuple.29, (bf16[128,8192]{1,0:T(8,128)(2,1)S(1)}, s32[1,1,2,64]{3,2,1,0:T(2,128)S(1)}, ...), branch_computations={%region_2.3_spmd, %region_3.6_spmd} | conditional | flops 285219200 | bytes 262150464 | solution.py:266
  175.5 3.3 %combine.2 = bf16[128,8192]{1,0:T(8,128)(2,1)} custom-call(s32[8,128]{1,0:T(8,128)S(1)} %get-tuple-element.22.refs_0_, bf16[128,8192]{1,0:T(8,128)(2,1)S(1)} %get-tuple-element.23.refs_1_, bf16[8,16,64,128]{3,2,1,0:T(8,128)(2,1)} %get-tuple-element.24.refs_2_, bf16[128,8192]{1,0:T(8,128)(2,1)} %get-tuple-element.25.refs_3_), custom_call_target="tpu_custom_call", output_to_operand_aliasing={{}: (3, {})} | custom-call | flops 2097152 | bytes 4194304 | tf_op jit(solution)/shard_map/cond/branch_0_fun/combine/pallas_call | solution.py:239
  (6 shorter events, 0.0 us)
Async XLA Ops:
  8.1 11.8 %all-to-all-start = ((s32[4,1,128]{2,1,0:T(1,128)}), s32[4,1,128]{2,1,0:T(1,128)S(1)}, u32[]{:S(2)}, u32[]{:S(2)}) async-start(s32[4,1,128]{2,1,0:T(1,128)} %bitcast.67), calls=%async_computation.1 | async-start | bytes 4096 | tf_op jit(solution)/shard_map/all_to_all | solution.py:193
  19.9 6.3 %copy-start.3 = (s32[4,1,128]{2,1,0:T(1,128)}, s32[4,1,128]{2,1,0:T(1,128)S(1)}, u32[]{:S(2)}) copy-start(s32[4,1,128]{2,1,0:T(1,128)S(1)} %all-to-all-done) | copy-start | bytes 6148
  22.6 8.4 %all-to-all-start.1 = ((s32[8,1,128]{2,1,0:T(1,128)}), s32[8,1,128]{2,1,0:T(1,128)S(1)}, u32[]{:S(2)}, u32[]{:S(2)}) async-start(s32[8,1,128]{2,1,0:T(1,128)} %bitcast.13), calls=%async_computation.2 | async-start | bytes 8192 | tf_op jit(solution)/shard_map/all_to_all | solution.py:214
  29.0 6.3 %copy-start = (bf16[128,8192]{1,0:T(8,128)(2,1)S(1)}, bf16[128,8192]{1,0:T(8,128)(2,1)}, u32[]{:S(2)}) copy-start(bf16[128,8192]{1,0:T(8,128)(2,1)} %refs_1_.5) | copy-start | bytes 6291460
  30.9 41.6 %all-to-all-start.4 = ((bf16[4,24,64,128]{3,2,1,0:T(8,128)(2,1)}), bf16[4,24,64,128]{3,2,1,0:T(8,128)(2,1)}, u32[]{:S(2)}, u32[]{:S(2)}) async-start(bf16[4,24,64,128]{3,2,1,0:T(8,128)(2,1)} %pack.3), calls=%async_computation.5 | async-start | bytes 3145728 | tf_op jit(solution)/shard_map/all_to_all | solution.py:210
  72.6 40.9 %all-to-all-start.2 = ((bf16[4,24,64,128]{3,2,1,0:T(8,128)(2,1)}), bf16[4,24,64,128]{3,2,1,0:T(8,128)(2,1)}, u32[]{:S(2)}, u32[]{:S(2)}) async-start(bf16[4,24,64,128]{3,2,1,0:T(8,128)(2,1)} %pack.2), calls=%async_computation.3 | async-start | bytes 3145728 | tf_op jit(solution)/shard_map/all_to_all | solution.py:210
  113.5 31.0 %all-to-all-start.5 = ((bf16[8,16,64,128]{3,2,1,0:T(8,128)(2,1)}), bf16[8,16,64,128]{3,2,1,0:T(8,128)(2,1)}, u32[]{:S(2)}, u32[]{:S(2)}) async-start(bf16[8,16,64,128]{3,2,1,0:T(8,128)(2,1)} %product.3), calls=%async_computation.6 | async-start | bytes 4194304 | tf_op jit(solution)/shard_map/all_to_all | solution.py:235
  144.5 31.0 %all-to-all-start.3 = ((bf16[8,16,64,128]{3,2,1,0:T(8,128)(2,1)}), bf16[8,16,64,128]{3,2,1,0:T(8,128)(2,1)}, u32[]{:S(2)}, u32[]{:S(2)}) async-start(bf16[8,16,64,128]{3,2,1,0:T(8,128)(2,1)} %product.2), calls=%async_computation.4 | async-start | bytes 4194304 | tf_op jit(solution)/shard_map/all_to_all | solution.py:235
  150.2 25.3 %copy-start.4 = (s32[1,1,2,64]{3,2,1,0:T(2,128)S(1)}, s32[1,1,2,64]{3,2,1,0:T(2,128)}, u32[]{:S(2)}) copy-start(s32[1,1,2,64]{3,2,1,0:T(2,128)} %refs_0_.1) | copy-start | bytes 1540

commit v3 on v0

v3 whole, which is shorter than its diff:
```python
import jax
import jax.numpy as jnp
from jax import lax
from jax.experimental import pallas as pl
from jax.experimental.pallas import tpu as pltpu
from jax.sharding import PartitionSpec as P

LEVELS = ((28, 16, 14), (28, 18, 14), (28, 20, 16), (32, 24, 20))
PARTS = (64, 32, 32)
SHIFT = 1024
VMEM_LIMIT = 60 * 1024 * 1024


def smem():
    return pl.BlockSpec(memory_space=pltpu.SMEM)


def anywhere():
    return pl.BlockSpec(memory_space=pl.ANY)


def one(shape, at=None):
    at = (0,) * len(shape) if at is None else at
    return pl.BlockSpec(shape, lambda i: at)


def pairs(n, t):
    return [(i, i ^ t) for i in range(n)]


def number(index, per_piece, owner_of, n_owner, wide):
    slots = index.shape[1]
    f32 = jnp.float32
    lane = lax.broadcasted_iota(jnp.int32, (slots, slots), 1)
    sub = lax.broadcasted_iota(jnp.int32, (slots, slots), 0)
    key_r = index.astype(f32)
    key_c = jnp.sum(jnp.where(lane == sub, key_r, 0.0), axis=1, keepdims=True)
    index_c = jnp.maximum(key_c.astype(jnp.int32), 0)
    owner_r = owner_of(jnp.maximum(index, 0)).astype(f32)
    owner_c = owner_of(index_c).astype(f32)
    local_c = lax.rem(index_c, per_piece).astype(f32)
    same = jnp.where(key_c == key_r, 1.0, 0.0)
    before = jnp.where(lane < sub, 1.0, 0.0)
    after = jnp.where(sub < lane, 1.0, 0.0)
    kin = jnp.where(owner_c == owner_r, 1.0, 0.0)
    first_c = jnp.where(jnp.sum(same * before, axis=1, keepdims=True) == 0.0, 1.0, 0.0)
    first_c = jnp.where(key_c >= 0.0, first_c, 0.0)
    first_r = jnp.where(jnp.sum(same * after, axis=0, keepdims=True) == 0.0, 1.0, 0.0)
    first_r = jnp.where(key_r >= 0.0, first_r, 0.0)
    rank_c = jnp.sum(kin * before * first_r, axis=1, keepdims=True)
    rank_r = jnp.sum(same * (first_c * rank_c), axis=0, keepdims=True)
    lanes = lax.broadcasted_iota(jnp.int32, (slots, wide), 1).astype(f32)
    spot = jnp.where(lanes == rank_c + 1.0, local_c, 0.0) + jnp.where(lanes == 0.0, 1.0, 0.0)
    rows = []
    for owner in range(n_owner):
        mine = first_c * jnp.where(owner_c == float(owner), 1.0, 0.0)
        rows.append(jnp.sum(spot * mine, axis=0, keepdims=True))
    return owner_r.astype(jnp.int32), rank_r.astype(jnp.int32), first_r, rows


def ask_kernel(n_row, n_col, per_piece, levels, index, line, places):
    wide = line.shape[1]
    k, j = index[0, 0, 0:1, :], index[0, 0, 1:2, :]
    from_r, from_rank, _, asks = number(
        k, per_piece, lambda v: lax.div(v, per_piece * n_col), n_row, wide
    )
    to_r, to_rank, first, lists = number(
        j, per_piece, lambda v: lax.rem(lax.div(v, per_piece), n_col), n_col, wide
    )
    row = lax.axis_index("row")
    need = jnp.zeros((1, 1), jnp.float32)
    for near, far, col in levels:
        over = jnp.zeros((1, 1), jnp.float32)
        for owner, ask in enumerate(asks):
            cap = jnp.where((owner ^ row) <= 1, float(near), float(far))
            over = jnp.maximum(over, jnp.where(ask[:, 0:1] > cap, 1.0, 0.0))
        for item in lists:
            over = jnp.maximum(over, jnp.where(item[:, 0:1] > float(col), 1.0, 0.0))
        need = need + over
    lane = lax.broadcasted_iota(jnp.int32, (1, wide), 1)
    told = jnp.concatenate(lists, axis=0) * float(SHIFT)
    for owner, ask in enumerate(asks):
        values = jnp.where(lane == wide - 1, need, ask + told)
        line[owner * n_col : (owner + 1) * n_col, :] = values.astype(jnp.int32)
    alive = jnp.where(j >= 0, 1.0, 0.0)
    live = jnp.sum(alive, axis=1, keepdims=True)
    places[0:1, :] = from_r ^ row
    places[1:2, :] = from_rank
    places[2:3, :] = to_r
    places[3:4, :] = to_rank
    places[4:5, :] = first.astype(jnp.int32)
    places[5:6, :] = jnp.broadcast_to(live, j.shape).astype(jnp.int32)


def fetch(copies):
    for copy in copies:
        copy.start()
    for copy in copies:
        copy.wait()


def pack_kernel(n_row, n_col, blk, heard, slab, *refs):
    packs, (asks, sems) = refs[:n_row], refs[n_row:]
    row, col = lax.axis_index("row"), lax.axis_index("col")
    fetch(
        [
            pltpu.make_async_copy(heard.at[(row ^ t) * n_col + col], asks.at[t], sems.at[t])
            for t in range(n_row)
        ]
    )
    for t in range(n_row):

        def copy(i, carry):
            at = pl.multiple_of((asks[t, 0, 1 + i] & (SHIFT - 1)) * blk, blk)
            packs[t][i] = slab[:, pl.ds(at, blk)]
            return carry

        lax.fori_loop(0, asks[t, 0, 0] & (SHIFT - 1), copy, 0)


def product_kernel(n_row, base, group, places, stored, *refs):
    panels = refs[:n_row]
    sums, held, total, sems = refs[n_row:]
    n_col, cap = sums.shape[:2]
    fetch(
        [
            pltpu.make_async_copy(panel, held.at[pl.ds(base[t], panel.shape[0])], sems.at[t])
            for t, panel in enumerate(panels)
        ]
    )
    live = places[5, 0]

    def start(t):
        at = jnp.int32(base[0])
        for i in range(1, n_row):
            at = jnp.where(t == i, base[i], at)
        return at

    def step(g, carry):
        products = []
        for u in range(group):
            s = g * group + u
            here = start(places[0, s]) + places[1, s]
            products.append(jnp.dot(held[here], stored[s], preferred_element_type=jnp.float32))
        for u in range(group):
            s = g * group + u
            o = jnp.where(s < live, places[2, s] * cap + places[3, s], n_col * cap)
            total[o] = jnp.where(places[4, s] == 1, 0.0, total[o]) + products[u]
        return carry

    lax.fori_loop(0, lax.div(live + group - 1, group), step, 0)

    def store(s, carry):
        @pl.when(places[4, s] == 1)
        def _():
            to, at = places[2, s], places[3, s]
            sums[to, at] = total[to * cap + at].astype(jnp.bfloat16)

        return carry

    lax.fori_loop(0, live, store, 0)


def combine_kernel(n_row, n_col, blk, heard, slab, sums, *refs):
    out, total, lists, sems = refs[-4:]
    row = lax.axis_index("row")
    copies = [
        pltpu.make_async_copy(heard.at[row * n_col + t], lists.at[t], sems.at[t])
        for t in range(n_col)
    ]
    for copy in copies:
        copy.start()
    total[...] = jnp.zeros_like(total)
    for copy in copies:
        copy.wait()
    for t in range(n_col):

        def add(i, carry):
            total[lists[t, 0, 1 + i] >> 10] += sums[t, i].astype(jnp.float32)
            return carry

        lax.fori_loop(0, lists[t, 0, 0] >> 10, add, 0)
    for i in range(out.shape[1] // blk):
        here = pl.ds(i * blk, blk)
        out[:, here] = (3.0 * slab[:, here].astype(jnp.float32) - 2.0 * total[i]).astype(out.dtype)


def exchange(heard, places, s_slab, stored, caps_in, cap, parts):
    blk = s_slab.shape[0]
    width = s_slab.shape[1]
    n_row = lax.axis_size("row")
    n_col = lax.axis_size("col")
    slots = stored.shape[0]
    group = 4 if slots % 4 == 0 else 1
    base = [sum(caps_in[:t]) for t in range(n_row)]
    params = pltpu.CompilerParams(vmem_limit_bytes=VMEM_LIMIT)
    firsts = [sum(parts[:i]) for i in range(len(parts))]
    result = None
    packed = [
        pl.pallas_call(
            lambda *refs: pack_kernel(n_row, n_col, blk, *refs),
            grid=(1,),
            out_shape=[jax.ShapeDtypeStruct((c, rows, blk), jnp.bfloat16) for c in caps_in],
            in_specs=[anywhere(), one((rows, width), (first // rows, 0))],
            out_specs=[one((c, rows, blk)) for c in caps_in],
            scratch_shapes=[
                pltpu.SMEM((n_row,) + heard.shape[1:], jnp.int32),
                pltpu.SemaphoreType.DMA((n_row,)),
            ],
            compiler_params=params,
            cost_estimate=pl.CostEstimate(
                flops=0, bytes_accessed=4 * rows * width, transcendentals=0
            ),
            name="pack",
        )(heard, s_slab)
        for first, rows in zip(firsts, parts)
    ]
    for first, rows, packs in zip(firsts, parts, packed):
        panels = [packs[0]] + [
            lax.ppermute(packs[t], "row", pairs(n_row, t)) for t in range(1, n_row)
        ]
        sums = pl.pallas_call(
            lambda *refs: product_kernel(n_row, base, group, *refs),
            grid=(1,),
            out_shape=jax.ShapeDtypeStruct((n_col, cap, rows, blk), jnp.bfloat16),
            in_specs=[smem(), one(stored.shape)] + [anywhere()] * n_row,
            out_specs=one((n_col, cap, rows, blk)),
            scratch_shapes=[
                pltpu.VMEM((sum(caps_in), rows, blk), jnp.bfloat16),
                pltpu.VMEM((n_col * cap + 1, rows, blk), jnp.float32),
                pltpu.SemaphoreType.DMA((n_row,)),
            ],
            compiler_params=params,
            cost_estimate=pl.CostEstimate(
                flops=2 * slots * rows * blk * blk,
                bytes_accessed=2 * blk * blk * slots + 2 * rows * blk * (sum(caps_in) + n_col * cap),
                transcendentals=0,
            ),
            name="product",
        )(places, stored, *panels)
        sums = lax.all_to_all(sums, "col", 0, 0, tiled=True)
        extra = [] if result is None else [result]
        result = pl.pallas_call(
            lambda *refs: combine_kernel(n_row, n_col, blk, *refs),
            grid=(1,),
            out_shape=jax.ShapeDtypeStruct(s_slab.shape, s_slab.dtype),
            in_specs=[
                anywhere(),
                one((rows, width), (first // rows, 0)),
                one((n_col, cap, rows, blk)),
            ]
            + [anywhere()] * len(extra),
            out_specs=one((rows, width), (first // rows, 0)),
            scratch_shapes=[
                pltpu.VMEM((width // blk, rows, blk), jnp.float32),
                pltpu.SMEM((n_col,) + heard.shape[1:], jnp.int32),
                pltpu.SemaphoreType.DMA((n_col,)),
            ],
            input_output_aliases={3: 0} if extra else {},
            compiler_params=params,
            cost_estimate=pl.CostEstimate(
                flops=4 * rows * width,
                bytes_accessed=4 * rows * width + 2 * rows * blk * n_col * cap,
                transcendentals=0,
            ),
            name="combine",
        )(heard, s_slab, sums, *extra)
    return result


def body(s_slab, p_blocks, p_index):
    blk = s_slab.shape[0]
    per_piece = s_slab.shape[1] // blk
    n_row = lax.axis_size("row")
    n_col = lax.axis_size("col")
    slots = p_blocks.shape[2]
    stored = p_blocks[0, 0]
    full = min(per_piece, slots)
    wide = -(-(2 + full) // 128) * 128
    parts = PARTS if sum(PARTS) == blk else (blk,)
    levels = [level for level in LEVELS if max(level) < full]
    levels.append((full, full, full))

    line, places = pl.pallas_call(
        lambda *refs: ask_kernel(n_row, n_col, per_piece, levels[:-1], *refs),
        out_shape=[
            jax.ShapeDtypeStruct((n_row * n_col, wide), jnp.int32),
            jax.ShapeDtypeStruct((6, slots), jnp.int32),
        ],
        name="ask",
    )(p_index)
    heard = lax.all_to_all(line, ("row", "col"), 0, 0, tiled=True)
    lines = heard.reshape(n_row * n_col, 1, wide)

    def run(level):
        near, far, cap = level
        caps_in = [near, near] + [far] * (n_row - 2)
        return lambda: exchange(lines, places, s_slab, stored, caps_in, cap, parts)

    if len(levels) == 1:
        return run(levels[0])()
    return lax.switch(jnp.max(heard[:, wide - 1]), [run(level) for level in levels])


def solution(mesh):
    placed = (
        P(None, ("row", "col")),
        P("row", "col", None, None, None),
        P("row", "col", None, None),
    )
    return jax.shard_map(
        body, mesh=mesh, in_specs=placed, out_specs=P(None, ("row", "col")), check_vma=False
    )
```

time: 368 us -> 144 us (0.39)
  waiting for transfers between devices: 267 us -> 56.3 us
  other arithmetic: 39.9 us -> 0.71 us
  local copies, waits for them, and re-layouts: 42.6 us -> 4.11 us
  starting transfers between devices: 0.04 us -> 34.9 us
  Pallas kernels: 0 us -> 34.2 us
  blocking collectives: 0 us -> 14.4 us
  between operations: 13.4 us -> 0.84 us
  matrix products: 4.41 us -> 0 us
    all_gather x1 -> x0, waiting for transfers between devices: 152 us -> none  [body(): gathered = lax.all_gather(s_slab, 'row', axis=1, tiled=True)]
    reduce_scatter x1 -> x0, waiting for transfers between devices: 115 us -> none  [body(): lax.psum_scatter(lax.fori_loop(0, slots // group, add_group, start).astyp...]
    ppermute x0 -> x9, waiting for transfers between devices: none -> 48 us  [exchange(): lax.ppermute(packs[t], 'row', pairs(n_row, t))]
    pallas_call x0 -> x10, Pallas kernels: none -> 34.2 us  [the longest x3 15.6 us: exchange(): pl.pallas_call(lambda *refs: product_kernel(n_row, base, group, *refs), g...]
    convert_element_type x2 -> x0, other arithmetic: 22.6 us -> none  [the longest x1 17.7 us: body(): lax.fori_loop(0, slots // group, add_group, start).astype(jnp.bfloat16)]
    ppermute x0 -> x9, starting transfers between devices: none -> 18.6 us  [exchange(): lax.ppermute(packs[t], 'row', pairs(n_row, t))]
    all_to_all x0 -> x3, starting transfers between devices: none -> 16.3 us  [exchange(): sums = lax.all_to_all(sums, 'col', 0, 0, tiled=True)]
    all_to_all x0 -> x1, blocking collectives: none -> 14.4 us  [body(): heard = lax.all_to_all(line, ('row', 'col'), 0, 0, tiled=True)]
  transfers between devices with their start and end apart: 2 -> 12, of which waited for: 2 -> 5; matrix products, arithmetic and copies ran while one was open for 0% -> 0% of each run, Pallas kernels for 0% -> 15%
where the time goes in v3:
time: 144 us; the launch traced here: 146 us
  waiting for transfers between devices  56.3 us (39%)
  starting transfers between devices  34.9 us (24%)
  Pallas kernels  34.2 us (24%)
  blocking collectives  14.4 us (10%)
  local copies, waits for them, and re-layouts  4.11 us (3%)
    ppermute x9, waiting for transfers between devices, exchange(): lax.ppermute(packs[t], 'row', pairs(n_row, t))  48 us
    ppermute x9, starting transfers between devices, exchange(): lax.ppermute(packs[t], 'row', pairs(n_row, t))  18.6 us
    all_to_all x3, starting transfers between devices, exchange(): sums = lax.all_to_all(sums, 'col', 0, 0, tiled=True)  16.3 us
    pallas_call x3, Pallas kernels, exchange(): pl.pallas_call(lambda *refs: product_kernel(n_row, base, group, *refs), g...  15.6 us
    all_to_all x1, blocking collectives, body(): heard = lax.all_to_all(line, ('row', 'col'), 0, 0, tiled=True)  14.4 us
    pallas_call x3, Pallas kernels, exchange(): pl.pallas_call(lambda *refs: combine_kernel(n_row, n_col, blk, *refs), gr...  10.4 us
    all_to_all x3, waiting for transfers between devices, exchange(): sums = lax.all_to_all(sums, 'col', 0, 0, tiled=True)  8.22 us
    pallas_call x3, Pallas kernels, exchange(): pl.pallas_call(lambda *refs: pack_kernel(n_row, n_col, blk, *refs), grid=...  6.54 us
  transfers between devices with their start and end apart: 12, of which 5 were waited for; matrix products, arithmetic and copies ran while one was open for 0% of the time, Pallas kernels for 15%

profile of v3, /device:TPU:0, one launch (start us, length us, event | category | flops | bytes accessed | tf_op | source)
XLA Modules:
  0.0 145.8 jit_solution(9446266342560104711)
XLA Ops:
  1.7 14.4 %all_to_all.72 = s32[32,1,128]{2,1,0:T(1,128)S(1)} all-to-all(s32[32,1,128]{2,1,0:T(1,128)} %bitcast.25), channel_id=1, replica_groups=mesh['row'=4,'col'=8] {'row','col'}, dimensions={0} | all-to-all | bytes 32768 | tf_op jit(solution)/shard_map/all_to_all | solution.py:292
  17.4 128.2 %conditional.1 = (bf16[128,8192]{1,0:T(8,128)(2,1)}) conditional(s32[]{:T(128)} %clamp.3, (s32[32,1,128]{2,1,0:T(1,128)S(1)}, bf16[128,8192]{1,0:T(8,128)(2,1)}, s32[6,64]{1,0:T(8,128)S(1)}, bf16[1,1,64,128,128]{4,3,2,1,0:T(8,128)(2,1)}) %tuple.20, (s32[32,1,128]{2,1,0:T(1,128)S(1)}, bf16[128,8192]{1,0:T(8,128)(2,1)}, ...), branch_computations={%region_1.0_spmd, %region_2.0_spmd, %region_3.0_spmd, %region_4.0_... | conditional | flops 272629760 | bytes 165675712 | solution.py:302
  17.4 2.8 %pack.22 = (bf16[28,32,128]{2,1,0:T(8,128)(2,1)}, bf16[28,32,128]{2,1,0:T(8,128)(2,1)}, bf16[20,32,128]{2,1,0:T(8,128)(2,1)}, bf16[20,32,128]{2,1,0:T(8,128)(2,1)}) custom-call(s32[32,1,128]{2,1,0:T(1,128)S(1)} %get-tuple-element.83.refs_0_, bf16[128,8192]{1,0:T(8,128)(2,1)} %get-tuple-element.148.refs_1_), custom_call_target="tpu_custom_call" | custom-call | bytes 1048576 | tf_op jit(solution)/shard_map/cond/branch_2_fun/pack/pallas_call | solution.py:200
  21.4 3.2 %collective-permute-start.23 = (bf16[20,32,128]{2,1,0:T(8,128)(2,1)}, bf16[20,32,128]{2,1,0:T(8,128)(2,1)S(1)}, u32[]{:S(2)}, u32[]{:S(2)}) collective-permute-start(bf16[20,32,128]{2,1,0:T(8,128)(2,1)} %get-tuple-element.94), channel_id=1, source_target_pairs={{0,24},{8,16},{16,8},{24,0},{1,25},{9,17},{17,9},{25,1},{2,26},{10... | collective-permute-start | bytes 491528 | tf_op jit(solution)/shard_map/cond/branch_2_fun/ppermute | solution.py:220
  24.6 11.5 %collective-permute-done.22.refs_4_ = bf16[20,32,128]{2,1,0:T(8,128)(2,1)S(1)} collective-permute-done((bf16[20,32,128]{2,1,0:T(8,128)(2,1)}, bf16[20,32,128]{2,1,0:T(8,128)(2,1)S(1)}, u32[]{:S(2)}, u32[]{:S(2)}) %collective-permute-start.22) | collective-permute-done | bytes 163872 | tf_op jit(solution)/shard_map/cond/branch_2_fun/ppermute | solution.py:220
  36.9 5.1 %product.22 = bf16[8,16,32,128]{3,2,1,0:T(8,128)(2,1)} custom-call(s32[6,64]{1,0:T(8,128)S(1)} %get-tuple-element.85.refs_0_, bf16[64,128,128]{2,1,0:T(8,128)(2,1)} %bitcast.15, bf16[28,32,128]{2,1,0:T(8,128)(2,1)} %get-tuple-element.91.refs_2_, bf16[28,32,128]{2,1,0:T(8,128)(2,1)} %copy-done.40, bf16[20,32,128]{2,1,0:T(8,128)(2,1)} %copy-done.46, ...), custom_call_target="tpu_custom_call" | custom-call | flops 67108864 | bytes 3932160 | tf_op jit(solution)/shard_map/cond/branch_2_fun/product/pallas_call | solution.py:222
  42.0 4.6 %all-to-all-start.7 = ((bf16[8,16,32,128]{3,2,1,0:T(8,128)(2,1)}), bf16[8,16,32,128]{3,2,1,0:T(8,128)(2,1)S(1)}, u32[]{:S(2)}, u32[]{:S(2)}) async-start(bf16[8,16,32,128]{3,2,1,0:T(8,128)(2,1)} %product.22), calls=%async_computation.7 | async-start | bytes 2097152 | tf_op jit(solution)/shard_map/cond/branch_2_fun/all_to_all | solution.py:241
  46.7 2.0 %pack.23 = (bf16[28,64,128]{2,1,0:T(8,128)(2,1)}, bf16[28,64,128]{2,1,0:T(8,128)(2,1)}, bf16[20,64,128]{2,1,0:T(8,128)(2,1)}, bf16[20,64,128]{2,1,0:T(8,128)(2,1)}) custom-call(s32[32,1,128]{2,1,0:T(1,128)S(1)} %get-tuple-element.83.refs_0_, bf16[128,8192]{1,0:T(8,128)(2,1)S(1)} %copy-done.2), custom_call_target="tpu_custom_call" | custom-call | bytes 2097152 | tf_op jit(solution)/shard_map/cond/branch_2_fun/pack/pallas_call | solution.py:200
  48.7 2.8 %collective-permute-start.24 = (bf16[28,64,128]{2,1,0:T(8,128)(2,1)}, bf16[28,64,128]{2,1,0:T(8,128)(2,1)S(1)}, u32[]{:S(2)}, u32[]{:S(2)}) collective-permute-start(bf16[28,64,128]{2,1,0:T(8,128)(2,1)} %get-tuple-element.96), channel_id=1, source_target_pairs={{0,8},{8,0},{16,24},{24,16},{1,9},{9,1},{17,25},{25,17},{2,10},{10... | collective-permute-start | bytes 1376264 | tf_op jit(solution)/shard_map/cond/branch_2_fun/ppermute | solution.py:220
  51.6 2.4 %collective-permute-start.26 = (bf16[20,64,128]{2,1,0:T(8,128)(2,1)}, bf16[20,64,128]{2,1,0:T(8,128)(2,1)S(1)}, u32[]{:S(2)}, u32[]{:S(2)}) collective-permute-start(bf16[20,64,128]{2,1,0:T(8,128)(2,1)} %get-tuple-element.98), channel_id=1, source_target_pairs={{0,24},{8,16},{16,8},{24,0},{1,25},{9,17},{17,9},{25,1},{2,26},{10... | collective-permute-start | bytes 983048 | tf_op jit(solution)/shard_map/cond/branch_2_fun/ppermute | solution.py:220
  54.0 15.8 %collective-permute-done.25.refs_4_ = bf16[20,64,128]{2,1,0:T(8,128)(2,1)S(1)} collective-permute-done((bf16[20,64,128]{2,1,0:T(8,128)(2,1)}, bf16[20,64,128]{2,1,0:T(8,128)(2,1)S(1)}, u32[]{:S(2)}, u32[]{:S(2)}) %collective-permute-start.25) | collective-permute-done | bytes 327712 | tf_op jit(solution)/shard_map/cond/branch_2_fun/ppermute | solution.py:220
  69.8 8.0 %collective-permute-done.26.refs_5_ = bf16[20,64,128]{2,1,0:T(8,128)(2,1)S(1)} collective-permute-done((bf16[20,64,128]{2,1,0:T(8,128)(2,1)}, bf16[20,64,128]{2,1,0:T(8,128)(2,1)S(1)}, u32[]{:S(2)}, u32[]{:S(2)}) %collective-permute-start.26) | collective-permute-done | bytes 327712 | tf_op jit(solution)/shard_map/cond/branch_2_fun/ppermute | solution.py:220
  79.3 5.5 %product.23 = bf16[8,16,64,128]{3,2,1,0:T(8,128)(2,1)} custom-call(s32[6,64]{1,0:T(8,128)S(1)} %get-tuple-element.85.refs_0_, bf16[64,128,128]{2,1,0:T(8,128)(2,1)} %bitcast.16, bf16[28,64,128]{2,1,0:T(8,128)(2,1)} %get-tuple-element.95.refs_2_, bf16[28,64,128]{2,1,0:T(8,128)(2,1)} %copy-done.25, bf16[20,64,128]{2,1,0:T(8,128)(2,1)} %copy-done.28, ...), custom_call_target="tpu_custom_call" | custom-call | flops 134217728 | bytes 5767168 | tf_op jit(solution)/shard_map/cond/branch_2_fun/product/pallas_call | solution.py:222
  84.9 5.9 %all-to-all-start.8 = ((bf16[8,16,64,128]{3,2,1,0:T(8,128)(2,1)}), bf16[8,16,64,128]{3,2,1,0:T(8,128)(2,1)}, u32[]{:S(2)}, u32[]{:S(2)}) async-start(bf16[8,16,64,128]{3,2,1,0:T(8,128)(2,1)} %product.23), calls=%async_computation.8 | async-start | bytes 4194304 | tf_op jit(solution)/shard_map/cond/branch_2_fun/all_to_all | solution.py:241
  90.7 1.8 %pack.21 = (bf16[28,32,128]{2,1,0:T(8,128)(2,1)}, bf16[28,32,128]{2,1,0:T(8,128)(2,1)}, bf16[20,32,128]{2,1,0:T(8,128)(2,1)}, bf16[20,32,128]{2,1,0:T(8,128)(2,1)}) custom-call(s32[32,1,128]{2,1,0:T(1,128)S(1)} %get-tuple-element.83.refs_0_, bf16[128,8192]{1,0:T(8,128)(2,1)S(1)} %copy-done.2), custom_call_target="tpu_custom_call" | custom-call | bytes 1048576 | tf_op jit(solution)/shard_map/cond/branch_2_fun/pack/pallas_call | solution.py:200
  92.5 6.4 %collective-permute-start.18 = (bf16[28,32,128]{2,1,0:T(8,128)(2,1)}, bf16[28,32,128]{2,1,0:T(8,128)(2,1)S(1)}, u32[]{:S(2)}, u32[]{:S(2)}) collective-permute-start(bf16[28,32,128]{2,1,0:T(8,128)(2,1)} %get-tuple-element.88), channel_id=1, source_target_pairs={{0,8},{8,0},{16,24},{24,16},{1,9},{9,1},{17,25},{25,17},{2,10},{10... | collective-permute-start | bytes 688136 | tf_op jit(solution)/shard_map/cond/branch_2_fun/ppermute | solution.py:220
  98.9 2.4 %collective-permute-start.20 = (bf16[20,32,128]{2,1,0:T(8,128)(2,1)}, bf16[20,32,128]{2,1,0:T(8,128)(2,1)S(1)}, u32[]{:S(2)}, u32[]{:S(2)}) collective-permute-start(bf16[20,32,128]{2,1,0:T(8,128)(2,1)} %get-tuple-element.90), channel_id=1, source_target_pairs={{0,24},{8,16},{16,8},{24,0},{1,25},{9,17},{17,9},{25,1},{2,26},{10... | collective-permute-start | bytes 491528 | tf_op jit(solution)/shard_map/cond/branch_2_fun/ppermute | solution.py:220
  101.3 12.8 %collective-permute-done.19.refs_4_ = bf16[20,32,128]{2,1,0:T(8,128)(2,1)S(1)} collective-permute-done((bf16[20,32,128]{2,1,0:T(8,128)(2,1)}, bf16[20,32,128]{2,1,0:T(8,128)(2,1)S(1)}, u32[]{:S(2)}, u32[]{:S(2)}) %collective-permute-start.19) | collective-permute-done | bytes 163872 | tf_op jit(solution)/shard_map/cond/branch_2_fun/ppermute | solution.py:220
  114.9 5.0 %product.21 = bf16[8,16,32,128]{3,2,1,0:T(8,128)(2,1)} custom-call(s32[6,64]{1,0:T(8,128)S(1)} %get-tuple-element.85.refs_0_, bf16[64,128,128]{2,1,0:T(8,128)(2,1)} %bitcast.17, bf16[28,32,128]{2,1,0:T(8,128)(2,1)} %get-tuple-element.87.refs_2_, bf16[28,32,128]{2,1,0:T(8,128)(2,1)} %copy-done.41, bf16[20,32,128]{2,1,0:T(8,128)(2,1)} %copy-done.47, ...), custom_call_target="tpu_custom_call" | custom-call | flops 67108864 | bytes 3932160 | tf_op jit(solution)/shard_map/cond/branch_2_fun/product/pallas_call | solution.py:222
  119.9 5.8 %all-to-all-start.6 = ((bf16[8,16,32,128]{3,2,1,0:T(8,128)(2,1)}), bf16[8,16,32,128]{3,2,1,0:T(8,128)(2,1)S(1)}, u32[]{:S(2)}, u32[]{:S(2)}) async-start(bf16[8,16,32,128]{3,2,1,0:T(8,128)(2,1)} %product.21), calls=%async_computation.6 | async-start | bytes 2097152 | tf_op jit(solution)/shard_map/cond/branch_2_fun/all_to_all | solution.py:241
  125.7 4.0 %combine.21.refs_3_ = bf16[128,8192]{1,0:T(8,128)(2,1)} custom-call(s32[32,1,128]{2,1,0:T(1,128)S(1)} %get-tuple-element.83.refs_0_, bf16[128,8192]{1,0:T(8,128)(2,1)S(1)} %copy-done.2, bf16[8,16,64,128]{3,2,1,0:T(8,128)(2,1)} %all-to-all-done.8.refs_2_), custom_call_target="tpu_custom_call" | custom-call | flops 2097152 | bytes 4194304 | tf_op jit(solution)/shard_map/cond/branch_2_fun/combine/pallas_call | solution.py:243
  129.7 3.2 %combine.22.refs_3_ = bf16[128,8192]{1,0:T(8,128)(2,1)} custom-call(s32[32,1,128]{2,1,0:T(1,128)S(1)} %get-tuple-element.83.refs_0_, bf16[128,8192]{1,0:T(8,128)(2,1)S(1)} %copy-done.2, bf16[8,16,32,128]{3,2,1,0:T(8,128)(2,1)} %copy-done.9, bf16[128,8192]{1,0:T(8,128)(2,1)} %combine.21.refs_3_), custom_call_target="tpu_custom_call", output_to_operand_aliasing={{}: (3, {})} | custom-call | flops 1048576 | bytes 2097152 | tf_op jit(solution)/shard_map/cond/branch_2_fun/combine/pallas_call | solution.py:243
  132.9 8.2 %all-to-all-done.6.refs_2_ = bf16[8,16,32,128]{3,2,1,0:T(8,128)(2,1)S(1)} async-done(((bf16[8,16,32,128]{3,2,1,0:T(8,128)(2,1)}), bf16[8,16,32,128]{3,2,1,0:T(8,128)(2,1)S(1)}, u32[]{:S(2)}, u32[]{:S(2)}) %all-to-all-start.6) | async-done | bytes 1048608 | tf_op jit(solution)/shard_map/cond/branch_2_fun/all_to_all | solution.py:241
  142.1 3.2 %combine.23 = bf16[128,8192]{1,0:T(8,128)(2,1)} custom-call(s32[32,1,128]{2,1,0:T(1,128)S(1)} %get-tuple-element.83.refs_0_, bf16[128,8192]{1,0:T(8,128)(2,1)S(1)} %copy-done.2, bf16[8,16,32,128]{3,2,1,0:T(8,128)(2,1)} %copy-done.10, bf16[128,8192]{1,0:T(8,128)(2,1)} %combine.22.refs_3_), custom_call_target="tpu_custom_call", output_to_operand_aliasing={{}: (3, {})} | custom-call | flops 1048576 | bytes 2097152 | tf_op jit(solution)/shard_map/cond/branch_2_fun/combine/pallas_call | solution.py:243
  (37 shorter events, 7.7 us)
Async XLA Ops:
  20.2 15.9 %collective-permute-start.21 = (bf16[28,32,128]{2,1,0:T(8,128)(2,1)}, bf16[28,32,128]{2,1,0:T(8,128)(2,1)S(1)}, u32[]{:S(2)}, u32[]{:S(2)}) collective-permute-start(bf16[28,32,128]{2,1,0:T(8,128)(2,1)} %get-tuple-element.92), channel_id=1, source_target_pairs={{0,8},{8,0},{16,24},{24,16},{1,9},{9,1},{17,25},{25,17},{2,10},{10... | collective-permute-start | bytes 688136 | tf_op jit(solution)/shard_map/cond/branch_2_fun/ppermute | solution.py:220
  20.9 15.3 %collective-permute-start.22 = (bf16[20,32,128]{2,1,0:T(8,128)(2,1)}, bf16[20,32,128]{2,1,0:T(8,128)(2,1)S(1)}, u32[]{:S(2)}, u32[]{:S(2)}) collective-permute-start(bf16[20,32,128]{2,1,0:T(8,128)(2,1)} %get-tuple-element.93), channel_id=1, source_target_pairs={{0,16},{8,24},{16,0},{24,8},{1,17},{9,25},{17,1},{25,9},{2,18},{10... | collective-permute-start | bytes 491528 | tf_op jit(solution)/shard_map/cond/branch_2_fun/ppermute | solution.py:220
  21.4 14.7 %collective-permute-start.23 = (bf16[20,32,128]{2,1,0:T(8,128)(2,1)}, bf16[20,32,128]{2,1,0:T(8,128)(2,1)S(1)}, u32[]{:S(2)}, u32[]{:S(2)}) collective-permute-start(bf16[20,32,128]{2,1,0:T(8,128)(2,1)} %get-tuple-element.94), channel_id=1, source_target_pairs={{0,24},{8,16},{16,8},{24,0},{1,25},{9,17},{17,9},{25,1},{2,26},{10... | collective-permute-start | bytes 491528 | tf_op jit(solution)/shard_map/cond/branch_2_fun/ppermute | solution.py:220
  36.1 0.7 copy-start.46
  36.1 0.7 copy-start.48
  36.1 0.8 copy-start.40
  36.9 9.8 %copy-start.2 = (bf16[128,8192]{1,0:T(8,128)(2,1)S(1)}, bf16[128,8192]{1,0:T(8,128)(2,1)}, u32[]{:S(2)}) copy-start(bf16[128,8192]{1,0:T(8,128)(2,1)} %get-tuple-element.148.refs_1_) | copy-start | bytes 6291460 | tf_op jit(solution)/shard_map/cond
  42.0 42.8 %all-to-all-start.7 = ((bf16[8,16,32,128]{3,2,1,0:T(8,128)(2,1)}), bf16[8,16,32,128]{3,2,1,0:T(8,128)(2,1)S(1)}, u32[]{:S(2)}, u32[]{:S(2)}) async-start(bf16[8,16,32,128]{3,2,1,0:T(8,128)(2,1)} %product.22), calls=%async_computation.7 | async-start | bytes 2097152 | tf_op jit(solution)/shard_map/cond/branch_2_fun/all_to_all | solution.py:241
  48.7 29.1 %collective-permute-start.24 = (bf16[28,64,128]{2,1,0:T(8,128)(2,1)}, bf16[28,64,128]{2,1,0:T(8,128)(2,1)S(1)}, u32[]{:S(2)}, u32[]{:S(2)}) collective-permute-start(bf16[28,64,128]{2,1,0:T(8,128)(2,1)} %get-tuple-element.96), channel_id=1, source_target_pairs={{0,8},{8,0},{16,24},{24,16},{1,9},{9,1},{17,25},{25,17},{2,10},{10... | collective-permute-start | bytes 1376264 | tf_op jit(solution)/shard_map/cond/branch_2_fun/ppermute | solution.py:220
  51.6 18.2 %collective-permute-start.25 = (bf16[20,64,128]{2,1,0:T(8,128)(2,1)}, bf16[20,64,128]{2,1,0:T(8,128)(2,1)S(1)}, u32[]{:S(2)}, u32[]{:S(2)}) collective-permute-start(bf16[20,64,128]{2,1,0:T(8,128)(2,1)} %get-tuple-element.97), channel_id=1, source_target_pairs={{0,16},{8,24},{16,0},{24,8},{1,17},{9,25},{17,1},{25,9},{2,18},{10... | collective-permute-start | bytes 983048 | tf_op jit(solution)/shard_map/cond/branch_2_fun/ppermute | solution.py:220
  51.6 26.2 %collective-permute-start.26 = (bf16[20,64,128]{2,1,0:T(8,128)(2,1)}, bf16[20,64,128]{2,1,0:T(8,128)(2,1)S(1)}, u32[]{:S(2)}, u32[]{:S(2)}) collective-permute-start(bf16[20,64,128]{2,1,0:T(8,128)(2,1)} %get-tuple-element.98), channel_id=1, source_target_pairs={{0,24},{8,16},{16,8},{24,0},{1,25},{9,17},{17,9},{25,1},{2,26},{10... | collective-permute-start | bytes 983048 | tf_op jit(solution)/shard_map/cond/branch_2_fun/ppermute | solution.py:220
  69.8 8.0 %copy-start.28 = (bf16[20,64,128]{2,1,0:T(8,128)(2,1)}, bf16[20,64,128]{2,1,0:T(8,128)(2,1)S(1)}, u32[]{:S(2)}) copy-start(bf16[20,64,128]{2,1,0:T(8,128)(2,1)S(1)} %collective-permute-done.25.refs_4_) | copy-start | bytes 983044 | tf_op jit(solution)/shard_map/cond
  77.8 0.7 copy-start.29
  78.5 0.8 copy-start.25
  84.8 7.6 %copy-start.9 = (bf16[8,16,32,128]{3,2,1,0:T(8,128)(2,1)}, bf16[8,16,32,128]{3,2,1,0:T(8,128)(2,1)S(1)}, u32[]{:S(2)}) copy-start(bf16[8,16,32,128]{3,2,1,0:T(8,128)(2,1)S(1)} %all-to-all-done.7.refs_2_) | copy-start | bytes 3145732 | tf_op jit(solution)/shard_map/cond
  84.9 35.0 %all-to-all-start.8 = ((bf16[8,16,64,128]{3,2,1,0:T(8,128)(2,1)}), bf16[8,16,64,128]{3,2,1,0:T(8,128)(2,1)}, u32[]{:S(2)}, u32[]{:S(2)}) async-start(bf16[8,16,64,128]{3,2,1,0:T(8,128)(2,1)} %product.23), calls=%async_computation.8 | async-start | bytes 4194304 | tf_op jit(solution)/shard_map/cond/branch_2_fun/all_to_all | solution.py:241
  92.5 21.6 %collective-permute-start.18 = (bf16[28,32,128]{2,1,0:T(8,128)(2,1)}, bf16[28,32,128]{2,1,0:T(8,128)(2,1)S(1)}, u32[]{:S(2)}, u32[]{:S(2)}) collective-permute-start(bf16[28,32,128]{2,1,0:T(8,128)(2,1)} %get-tuple-element.88), channel_id=1, source_target_pairs={{0,8},{8,0},{16,24},{24,16},{1,9},{9,1},{17,25},{25,17},{2,10},{10... | collective-permute-start | bytes 688136 | tf_op jit(solution)/shard_map/cond/branch_2_fun/ppermute | solution.py:220
  98.9 15.2 %collective-permute-start.19 = (bf16[20,32,128]{2,1,0:T(8,128)(2,1)}, bf16[20,32,128]{2,1,0:T(8,128)(2,1)S(1)}, u32[]{:S(2)}, u32[]{:S(2)}) collective-permute-start(bf16[20,32,128]{2,1,0:T(8,128)(2,1)} %get-tuple-element.89), channel_id=1, source_target_pairs={{0,16},{8,24},{16,0},{24,8},{1,17},{9,25},{17,1},{25,9},{2,18},{10... | collective-permute-start | bytes 491528 | tf_op jit(solution)/shard_map/cond/branch_2_fun/ppermute | solution.py:220
  98.9 15.2 %collective-permute-start.20 = (bf16[20,32,128]{2,1,0:T(8,128)(2,1)}, bf16[20,32,128]{2,1,0:T(8,128)(2,1)S(1)}, u32[]{:S(2)}, u32[]{:S(2)}) collective-permute-start(bf16[20,32,128]{2,1,0:T(8,128)(2,1)} %get-tuple-element.90), channel_id=1, source_target_pairs={{0,24},{8,16},{16,8},{24,0},{1,25},{9,17},{17,9},{25,1},{2,26},{10... | collective-permute-start | bytes 491528 | tf_op jit(solution)/shard_map/cond/branch_2_fun/ppermute | solution.py:220
  114.1 0.7 copy-start.47
  114.1 0.7 copy-start.49
  114.1 0.8 copy-start.41
  119.9 21.2 %all-to-all-start.6 = ((bf16[8,16,32,128]{3,2,1,0:T(8,128)(2,1)}), bf16[8,16,32,128]{3,2,1,0:T(8,128)(2,1)S(1)}, u32[]{:S(2)}, u32[]{:S(2)}) async-start(bf16[8,16,32,128]{3,2,1,0:T(8,128)(2,1)} %product.21), calls=%async_computation.6 | async-start | bytes 2097152 | tf_op jit(solution)/shard_map/cond/branch_2_fun/all_to_all | solution.py:241
  141.1 1.0 copy-start.10
